TPU v7x, 32 devices: a whole 2x2x4 slice. The times are simulated.
32 devices in a mesh: section: 2 (over core), batch: 16 (over z, y, x).
Axes of the slice: x: 2, y: 2, z: 4, core: 2. Of those that a mesh axis runs over, the one named last changes fastest.
Arguments:
- x_query: bfloat16 [128, 32, 768], P('batch'), may hold values from -6 to 6
- x_passage: bfloat16 [32, 256, 768], P('batch'), may hold values from -6 to 6
- len_query: int32 [128], P('batch'), may hold values from 16 to 32, as said below
- len_passage: int32 [32], P('batch'), may hold values from 33 to 256, as said below
- positive: int32 [128], P('batch'), may hold values from 0 to 31
- cot_query: bfloat16 [128, 32, 768], P('batch'), may hold values from -6 to 6
- cot_passage: bfloat16 [32, 256, 768], P('batch'), may hold values from -6 to 6
- w_qkv: bfloat16 [2, 768, 2304], P('section'), may hold values from -0.21875 to 0.21875
- b_qv: float32 [2, 1536], P('section'), may hold values from -3 to 3
- w_o: bfloat16 [2, 768, 768], P('section'), may hold values from -1.75 to 1.75
- b_o: float32 [2, 768], P('section'), may hold values from -3 to 3
- g_attn: float32 [2, 768], P('section'), may hold values from 0.5 to 1.5
- c_attn: float32 [2, 768], P('section'), may hold values from -2 to 2
- w_in: bfloat16 [2, 768, 3072], P('section'), may hold values from -0.21875 to 0.21875
- b_in: float32 [2, 3072], P('section'), may hold values from -3 to 3
- w_out: bfloat16 [2, 3072, 768], P('section'), may hold values from -0.109375 to 0.109375
- b_out: float32 [2, 768], P('section'), may hold values from -3 to 3
- g_ffn: float32 [2, 768], P('section'), may hold values from 0.5 to 1.5
- c_ffn: float32 [2, 768], P('section'), may hold values from -2 to 2
Outputs:
- hidden_query: bfloat16 [2, 128, 32, 768], P('section', 'batch')
- hidden_passage: bfloat16 [2, 32, 256, 768], P('section', 'batch')
- grad_query: float32 [2, 128, 32, 768], P('section', 'batch')
- grad_passage: float32 [2, 32, 256, 768], P('section', 'batch')
- loss_value: float32 [], replicated
- d_w_qkv: float32 [2, 768, 2304], P('section', 'batch')
- d_b_qv: float32 [2, 1536], P('section', 'batch')
- d_w_o: float32 [2, 768, 768], P('section', 'batch')
- d_b_o: float32 [2, 768], P('section', 'batch')
- d_g_attn: float32 [2, 768], P('section', 'batch')
- d_c_attn: float32 [2, 768], P('section', 'batch')
- d_w_in: float32 [2, 768, 3072], P('section', 'batch')
- d_b_in: float32 [2, 3072], P('section', 'batch')
- d_w_out: float32 [2, 3072, 768], P('section', 'batch')
- d_b_out: float32 [2, 768], P('section', 'batch')
- d_g_ffn: float32 [2, 768], P('section', 'batch')
- d_c_ffn: float32 [2, 768], P('section', 'batch')
Inputs may be any that keep to these rules, and one draw needn't show every extreme that they name: `len_query`: valid tokens of each query, from the start of its 32 slots; some query has exactly 32. `len_passage`: valid tokens of each passage, from the start of its 256 slots; most are short, some fill all 256; some passage has exactly 256.
All inputs are finite; a program needn't handle non-finite values.
Results may differ from a plain program's by a relative error of at most 0.028.
Values may be sent and summed in bfloat16 or wider, within the bound.
A program may use at most 256 MiB of HBM per device.

v0:
```python
import functools
import math

import jax
import jax.numpy as jnp
from jax import lax
from jax.experimental import pallas as pl
from jax.experimental.pallas import tpu as pltpu
from jax.sharding import PartitionSpec as P

HEADS = 12
QLEN = 32
PLEN = 256


norm_eps = 1e-05


def contrast(logits, targets):
    top_score = jnp.max(logits, -1, keepdims=True)
    log_total = top_score[:, 0] + jnp.log(jnp.sum(jnp.exp(logits - top_score), -1))
    chosen = targets[:, None] == jnp.arange(logits.shape[1])[None, :]
    term_values = log_total - jnp.sum(jnp.where(chosen, logits, 0.0), -1)
    grad_logits = (jnp.exp(logits - log_total[:, None]) - chosen.astype(jnp.float32)).astype(
        jnp.bfloat16
    )
    return (term_values, grad_logits)


MESH = pl.DeviceIdType.MESH
CHUNK = 384
COUNT = 12
BLOCK = 48


def swap(value):
    return lax.ppermute(value, "section", [(0, 1), (1, 0)])


LOW = jnp.bfloat16
FULL = jnp.float32
ROWS = 32
TILE = 768
LAST = (((1,), (1,)), ((), ()))
FIRST = (((0,), (0,)), ((), ()))


def dot(left, right):
    return jnp.dot(left, right, preferred_element_type=FULL)


def dot_last(left, right):
    return lax.dot_general(left, right, LAST, preferred_element_type=FULL)


def dot_first(left, right):
    return lax.dot_general(left, right, FIRST, preferred_element_type=FULL)


UNROLL = 4
PAIRS = 3


def over(count, body, unroll=1):
    def step(index, carry):
        body(index)
        return carry

    lax.fori_loop(0, count, step, 0, unroll=unroll)


def row_range(index):
    return pl.ds(pl.multiple_of(index * ROWS, ROWS), ROWS)


def lane_range(index, width):
    return pl.ds(pl.multiple_of(index * width, 128), width)


def moments(block):
    centred = block - jnp.mean(block, -1, keepdims=True)
    spread = jnp.mean(centred * centred, -1, keepdims=True)
    inverse = lax.rsqrt(spread + norm_eps)
    return centred * inverse, inverse


def gelu_pair(block):
    size = jnp.abs(block)
    t = 1.0 / (1.0 + (0.3275911 * math.sqrt(0.5)) * size)
    bell = jnp.exp(-0.5 * block * block)
    poly = 0.5 * 1.061405429
    for term in (-1.453152027, 1.421413741, -0.284496736, 0.254829592):
        poly = poly * t + 0.5 * term
    tail = poly * t * bell
    phi = jnp.where(block > 0, 1.0 - tail, tail)
    return block * phi, phi + block * bell * (1.0 / math.sqrt(2.0 * math.pi))


def head_lanes(rows, head):
    lane = lax.broadcasted_iota(jnp.int32, (rows, 128), 1)
    return (lane < 64) if head == 0 else (lane >= 64)


def query_mask(lens, start, count):
    rows = count * QLEN
    row = lax.broadcasted_iota(jnp.int32, (rows, rows), 0)
    column = lax.broadcasted_iota(jnp.int32, (rows, rows), 1)
    limit = jnp.zeros((rows, rows), jnp.int32)
    for item in range(count):
        limit = jnp.where(column // QLEN == item, item * QLEN + lens[start + item], limit)
    return (row // QLEN == column // QLEN) & (row < limit)


VMEM_LIMIT = 58 * 1024 * 1024


def remote(src, dst, send, recv, where):
    return pltpu.make_async_remote_copy(
        src_ref=src, dst_ref=dst, send_sem=send, recv_sem=recv,
        device_id=where, device_id_type=MESH,
    )


def greet(targets):
    barrier = pltpu.get_barrier_semaphore()
    for where in targets:
        pl.semaphore_signal(barrier, inc=1, device_id=where, device_id_type=MESH)
    pl.semaphore_wait(barrier, len(targets))


def forward_kernel(
    parts, x_query, x_passage, qlens, plens, positive,
    b_qv, b_o, g_attn, c_attn, b_in, b_out, g_ffn, c_ffn, wqkv, wo, win, wout,
    o_left, o_qkv, o_pq, o_pp, o_pre, o_slope, o_ffn, both_par,
    l_qkv, l_o, l_in, l_out, hid_q, hid_p, gcls, loss,
    tok, out, bqkv, bo, bin_, bout, qkv, pq, pp, mixed, pre, normed_full, normed, up, act,
    slope, ffn, rows8, rows48, packed, every, stack,
    load, save, xload, parsend, parrecv, wsend, wrecv, hsend, hrecv, hlocal, gsend, grecv, psend, precv,
):
    core = lax.axis_index("section")
    me = lax.axis_index("batch")
    peer = {"section": 1 - core}
    features = wo.shape[0]
    count_q, count_p = x_query.shape[0] // 2, x_passage.shape[0] // 2
    split = count_q * QLEN
    tall = count_p
    total = (count_q + count_p) * QLEN
    own = (wqkv, wo, win, wout)
    land = (l_qkv, l_o, l_in, l_out)
    buffers = (bqkv, bo, bin_, bout)

    gets = [
        pltpu.make_async_copy(
            x_query.at[pl.ds(core * count_q, count_q)], tok.at[0, pl.ds(0, count_q)], xload.at[0]
        ),
        pltpu.make_async_copy(
            x_passage.at[pl.ds(core * tall, tall)], tok.at[0, pl.ds(count_q, tall)], xload.at[1]
        ),
    ]
    for copy in gets:
        copy.start()

    def local(source, spot):
        return pltpu.make_async_copy(source[spot], buffers[spot], load.at[spot])

    def stash(spot):
        return pltpu.make_async_copy(buffers[spot], land[spot], load.at[4 + spot])

    def give_first(spot):
        return remote(own[spot], buffers[spot], wsend.at[spot], wrecv.at[spot], peer)

    def give_second(spot):
        return remote(own[spot], land[spot], wsend.at[spot], wrecv.at[spot], peer)

    others = [peer]
    if parts == 16:
        for step in range(1, parts):
            others.append({"batch": (me + step) % parts})

    @pl.when(core == 0)
    def _():
        for spot in range(4):
            local(own, spot).start()

    vectors = (b_qv, b_o, g_attn, c_attn, b_in, b_out, g_ffn, c_ffn)
    spot = 0
    for ref in vectors:
        for item in range(ref.shape[1] // features):
            both_par[core, spot : spot + 1] = ref[:, item * features : (item + 1) * features]
            spot += 1
    both_par[core, spot:16] = jnp.zeros((16 - spot, features), FULL)
    greet(others)
    give_par = remote(both_par.at[core], both_par.at[core], parsend, parrecv, peer)
    give_par.start()

    @pl.when(core == 0)
    def _():
        for spot in range(4):
            give_first(spot).start()

    @pl.when(core == 1)
    def _():
        for spot in range(4):
            give_second(spot).start()

    def weight_first(spot):
        @pl.when(core == 0)
        def _():
            local(own, spot).wait()

        @pl.when(core == 1)
        def _():
            give_first(spot).wait_recv()
            stash(spot).start()

    def fetch_second(spot):
        @pl.when(core == 0)
        def _():
            give_second(spot).wait_recv()
            local(land, spot).start()

        @pl.when(core == 1)
        def _():
            stash(spot).wait()
            local(own, spot).start()

    def weight(layer, spot):
        if layer == 0:
            weight_first(spot)
        else:
            local(own, spot).wait()

    saves = {}

    def keep(name, layer, source, target):
        saves[name, layer] = pltpu.make_async_copy(
            source, target, save.at[len(saves)]
        )
        saves[name, layer].start()

    def free(name, layer):
        if layer == 1:
            saves[name, 0].wait()

    for copy in gets:
        copy.wait()

    remote(both_par.at[core], both_par.at[1 - core], parsend, parrecv, peer).wait_recv()
    blocks = [(0, split, query_mask(qlens, core * count_q, count_q), pq, 0)]
    for item in range(count_p * QLEN // PLEN):
        row = lax.broadcasted_iota(jnp.int32, (PLEN, PLEN), 0)
        limit = plens[core * (count_p * QLEN // PLEN) + item]
        blocks.append((split + item * PLEN, PLEN, row < limit, pp, item * HEADS))

    for layer in (0, 1):
        base_row = 0
        par = both_par.at[layer]
        x = tok.at[layer].reshape(total, features)
        keep("tok", layer, x, o_left.at[layer, 6])
        weight(layer, 0)
        free("qkv", layer)

        def project(tile):
            lanes = lane_range(tile, features)
            bias = jnp.where(tile == 0, par[base_row : base_row + 1], 0.0)
            bias = jnp.where(tile == 2, par[base_row + 1 : base_row + 2], bias)
            qkv[:, lanes] = (dot(x[...], bqkv[:, lanes]) + bias).astype(LOW)

        over(3, project)
        keep("qkv", layer, qkv, o_qkv.at[layer])
        if layer == 1:
            fetch_second(3)
        for name in ("pq", "pp", "mixed"):
            free(name, layer)

        def attend(index):
            tasks = []
            for step in range(PAIRS):
                for lo, rows, mask, probs, base in blocks:
                    tasks.append((index * PAIRS + step, lo, rows, mask, probs, base))

            def part(task, offset):
                hp, lo, rows = task[:3]
                return qkv[pl.ds(lo, rows), pl.ds(pl.multiple_of(offset + hp * 128, 128), 128)]

            scores = []
            for task in tasks:
                queries, keys = part(task, 0) * LOW(0.125), part(task, features)
                for head in (0, 1):
                    masked = jnp.where(head_lanes(task[2], head), keys, LOW(0))
                    scores.append(dot_last(masked, queries))
            lows = []
            for spot, value in enumerate(scores):
                hp, lo, rows, mask, probs, base = tasks[spot // 2]
                value = jnp.where(mask, value, -1000000000.0)
                weights = jnp.exp(value - jnp.max(value, 0, keepdims=True))
                inverse = 1.0 / jnp.sum(weights, 0, keepdims=True)
                low = (weights * inverse).astype(LOW)
                probs[base + 2 * hp + spot % 2] = low
                lows.append(low)
            for spot, task in enumerate(tasks):
                hp, lo, rows = task[:3]
                values = part(task, 2 * features).T
                outs = [
                    dot(values[64 * head : 64 * head + 64], lows[2 * spot + head])
                    for head in (0, 1)
                ]
                both = jnp.concatenate(outs, 0).astype(LOW).T
                mixed[pl.ds(lo, rows), pl.ds(pl.multiple_of(hp * 128, 128), 128)] = both

        over(features // 128 // PAIRS, attend)
        keep("pq", layer, pq, o_pq.at[layer])
        keep("pp", layer, pp, o_pp.at[layer])
        keep("mixed", layer, mixed, o_left.at[layer, 5])
        weight(layer, 1)
        free("pre", layer)
        pre[...] = (
            dot(mixed[...], bo[...]) + x[...].astype(FULL) + par[base_row + 2 : base_row + 3]
        )
        keep("pre", layer, pre, o_pre.at[layer])
        if layer == 0:
            fetch_second(0)
            fetch_second(1)
        free("normed", layer)

        def norm_one(index):
            rows = row_range(index)
            block = moments(pre[rows])[0] * par[base_row + 3 : base_row + 4]
            block = block + par[base_row + 4 : base_row + 5]
            normed_full[rows] = block
            normed[rows] = block.astype(LOW)

        over(total // ROWS, norm_one, UNROLL)
        keep("normed", layer, normed, o_left.at[layer, 4])
        weight(layer, 2)
        for item in range(4):
            free("act%d" % item, layer)
        free("slope", layer)
        step_width = 256
        tiles = win.shape[1] // step_width

        def expand(tile):
            lanes = lane_range(tile, step_width)
            bias_lanes = lane_range(tile % 3, step_width)
            up[tile % 2] = (
                dot(normed[...], bin_[:, lanes])
                + par[pl.ds(base_row + 5 + tile // 3, 1), bias_lanes]
            )

        def bend(tile):
            lanes = lane_range(tile, step_width)
            for index in range(total // ROWS):
                rows = pl.ds(index * ROWS, ROWS)
                value, steep = gelu_pair(up[tile % 2, rows])
                act[rows, lanes] = value.astype(LOW)
                slope[rows, lanes] = steep.astype(LOW)

        expand(0)

        def grow(index):
            expand(index + 1)
            bend(index)

        over(tiles - 1, grow)
        bend(tiles - 1)
        for item in range(4):
            lanes = pl.ds(item * features, features)
            keep("act%d" % item, layer, act.at[:, lanes], o_left.at[layer, item])
        keep("slope", layer, slope, o_slope.at[layer])
        weight(layer, 3)
        free("ffn", layer)
        ffn[...] = (
            dot(act[...], bout[...]) + normed_full[...] + par[base_row + 9 : base_row + 10]
        )
        keep("ffn", layer, ffn, o_ffn.at[layer])
        if layer == 0:
            fetch_second(2)
        target = tok.at[1] if layer == 0 else out
        flat = target.reshape(total, features)

        def norm_two(index):
            rows = row_range(index)
            block = moments(ffn[rows])[0] * par[base_row + 10 : base_row + 11]
            flat[rows] = (block + par[base_row + 11 : base_row + 12]).astype(LOW)

        over(total // ROWS, norm_two, UNROLL)
        sides = (
            (target.at[pl.ds(0, count_q)], hid_q.at[pl.ds(core * count_q, count_q)]),
            (target.at[pl.ds(count_q, tall)], hid_p.at[pl.ds(core * tall, tall)]),
        )

        @pl.when(core == layer)
        def _():
            for spot, (src, dst) in enumerate(sides):
                pltpu.make_async_copy(src, dst, hlocal.at[spot]).start()

        @pl.when(core != layer)
        def _():
            for spot, (src, dst) in enumerate(sides):
                remote(src, dst, hsend.at[spot], hrecv.at[spot], peer).start()

    if parts == 16:
        lead = [item * QLEN for item in range(count_q)] + [split]
        rows8[...] = jnp.zeros_like(rows8)
        for spot, row in enumerate(lead):
            rows8[spot : spot + 1] = flat[pl.ds(row, 16)].astype(FULL)[0:1]
        for tile in range(6):
            rows48[8 * tile : 8 * tile + 8] = rows8[:, 128 * tile : 128 * tile + 128]
        for item in range(count_q):
            value = positive[core * count_q + item].astype(FULL)
            rows48[8 * item + 5 : 8 * item + 6] = jnp.full((1, 128), value)
        packed[...] = rows48[...].astype(LOW)

        def share(step, slot):
            return remote(
                packed, every.at[core, slot], gsend.at[step], grecv.at[slot],
                {"batch": (me + step) % parts},
            )

        for step in range(1, parts):
            share(step, me).start()
        every[core, me] = packed[...]
        for step in range(1, parts):
            share(step, (me + parts - step) % parts).wait_recv()
        pass_on = remote(every.at[core], every.at[core], psend, precv, peer)
        pass_on.start()
        remote(every.at[core], every.at[1 - core], psend, precv, peer).wait_recv()
        pass_on.wait_send()
        for step in range(1, parts):
            share(step, me).wait_send()

        wide = 2 * parts * 8
        grid = every[...].astype(FULL).reshape(2 * parts, 48, 128)
        inner = lax.broadcasted_iota(jnp.int32, (2 * parts, 8, 128), 1)
        goal = jnp.zeros((2 * parts, 8, 128), FULL)
        for tile in range(6):
            block = grid[:, 8 * tile : 8 * tile + 8]
            stack[:, 128 * tile : 128 * tile + 128] = block.reshape(wide, 128).astype(LOW)
            if tile < count_q:
                found = jnp.sum(jnp.where(inner == 5, block, 0.0), 1, keepdims=True)
                goal = jnp.where(inner == tile, found, goal)
        row = lax.broadcasted_iota(jnp.int32, (wide, wide), 0)
        column = lax.broadcasted_iota(jnp.int32, (wide, wide), 1)
        scale = 2.0 / math.sqrt(features)
        logits = dot_last(stack[...], stack[...]) * scale
        device = column // 8
        passage = (device % parts) * 2 + device // parts
        is_passage = column % 8 == count_q
        is_query = row % 8 < count_q
        kept = jnp.where(is_passage, logits, -1e30)
        top = jnp.max(kept, -1, keepdims=True)
        log_total = top + jnp.log(jnp.sum(jnp.exp(kept - top), -1, keepdims=True))
        chosen = is_passage & (passage.astype(FULL) == goal.reshape(wide, 128)[:, 0:1])
        picked = jnp.sum(jnp.where(chosen, logits, 0.0), -1, keepdims=True)
        terms = jnp.where(is_query[:, 0:1], log_total - picked, 0.0)
        count = count_q * 2 * parts
        loss[...] = jnp.full((8, 128), jnp.sum(terms) / count)
        grads = jnp.exp(kept - log_total) - chosen.astype(FULL)
        grads = jnp.where(is_query & is_passage, grads, 0.0)
        up[0, 0:wide, 0:wide] = grads + grads.T
        mine = pl.multiple_of((core * parts + me) * 8, 8)
        picked_rows = up[0, pl.ds(mine, 8), 0:wide]
        gcls[...] = dot(picked_rows.astype(LOW), stack[...]) * scale

    for spot, (src, dst) in enumerate(sides):
        pltpu.make_async_copy(src, dst, hlocal.at[spot]).wait()
    theirs = (
        hid_q.at[pl.ds((1 - core) * count_q, count_q)],
        hid_p.at[pl.ds((1 - core) * tall, tall)],
    )
    for spot, (src, dst) in enumerate(zip((item[0] for item in sides), theirs)):
        remote(src, dst, hsend.at[spot], hrecv.at[spot], peer).wait()
    for spot in range(4):
        give_second(spot).wait_send()
    give_par.wait_send()
    for (name, layer), copy in saves.items():
        if layer == 1:
            copy.wait()
    saves["tok", 0].wait()


def forward_both(parts, x_query, x_passage, qlens, plens, positive, vectors, own):
    queries, features = x_query.shape[0], x_query.shape[2]
    passages = x_passage.shape[0]
    total = (queries + passages) // 2 * QLEN
    wide = own[2].shape[1]
    split = queries // 2 * QLEN
    heads_p = HEADS * (passages // 2 * QLEN // PLEN)
    kept = [
        ((7, total, features), LOW),
        ((total, 3 * features), LOW),
        ((HEADS, split, split), LOW),
        ((heads_p, PLEN, PLEN), LOW),
        ((total, features), FULL),
        ((total, wide), LOW),
        ((total, features), FULL),
        ((16, features), FULL),
    ]
    shape = jax.ShapeDtypeStruct
    anywhere = pl.BlockSpec(memory_space=pl.ANY)
    vmem = pl.BlockSpec(memory_space=pltpu.VMEM)
    smem = pl.BlockSpec(memory_space=pltpu.SMEM)
    dma = pltpu.SemaphoreType.DMA
    scratch = [
        pltpu.VMEM((2, total // QLEN, QLEN, features), LOW),
        pltpu.VMEM((total // QLEN, QLEN, features), LOW),
    ]
    scratch += [pltpu.VMEM(item.shape, item.dtype) for item in own]
    scratch += [pltpu.VMEM(size, kind) for size, kind in kept[1:4]]
    scratch += [
        pltpu.VMEM((total, features), LOW),
        pltpu.VMEM((total, features), FULL),
        pltpu.VMEM((total, features), FULL),
        pltpu.VMEM((total, features), LOW),
        pltpu.VMEM((2, total, 256), FULL),
        pltpu.VMEM((total, wide), LOW),
        pltpu.VMEM((total, wide), LOW),
        pltpu.VMEM((total, features), FULL),
    ]
    scratch += [
        pltpu.VMEM((8, features), FULL),
        pltpu.VMEM((48, 128), FULL),
        pltpu.VMEM((48, 128), LOW),
        pltpu.VMEM((2, 16, 48, 128), LOW),
        pltpu.VMEM((256, features), LOW),
        dma((8,)),
        dma((26,)),
        dma((2,)),
        dma,
        dma,
        dma((4,)),
        dma((4,)),
        dma((2,)),
        dma((2,)),
        dma((2,)),
        dma((16,)),
        dma((16,)),
        dma,
        dma,
    ]
    return pl.pallas_call(
        functools.partial(forward_kernel, parts),
        out_shape=[shape((2,) + size, kind) for size, kind in kept]
        + [shape(item.shape, item.dtype) for item in own]
        + [
            shape(x_query.shape, LOW),
            shape(x_passage.shape, LOW),
            shape((8, features), FULL),
            shape((8, 128), FULL),
        ],
        in_specs=[anywhere, anywhere, smem, smem, smem] + [vmem] * 8 + [anywhere] * 4,
        out_specs=[anywhere] * 7 + [vmem] + [anywhere] * 6 + [vmem] * 2,
        scratch_shapes=scratch,
        compiler_params=pltpu.CompilerParams(
            collective_id=2, has_side_effects=True, vmem_limit_bytes=VMEM_LIMIT
        ),
    )(x_query, x_passage, qlens, plens, positive, *vectors, *own)


def add_rows(block):
    return jnp.sum(block.reshape(block.shape[0] // 8, 8, block.shape[1]), 0)


def norm_back(source, grad_of, gain, total, store):
    features = source.shape[1]
    zero = jnp.zeros((8, features), FULL)

    def step(index, carry):
        rows = row_range(index)
        grad = grad_of(index)
        unit, inverse = moments(source[rows])
        scaled = grad * gain
        back = inverse * (
            scaled
            - jnp.mean(scaled, -1, keepdims=True)
            - unit * jnp.mean(scaled * unit, -1, keepdims=True)
        )
        store(rows, back)
        return (
            carry[0] + add_rows(grad * unit),
            carry[1] + add_rows(grad),
            carry[2] + add_rows(back),
        )

    sums = lax.fori_loop(0, total // ROWS, step, (zero, zero, zero), unroll=UNROLL)
    return [jnp.sum(item, 0, keepdims=True) for item in sums]


def left_index(ch):
    return (
        jnp.minimum(ch, 4) + (ch >= 8).astype(jnp.int32) + (ch >= 9).astype(jnp.int32)
    )


def right_index(ch):
    return jnp.maximum(ch - 3, 0)


def backward_kernel(parts, *refs):
    small = parts == 16
    refs = list(refs)

    def take(count):
        front = refs[:count]
        del refs[:count]
        return front

    cot_query, cot_passage, qlens, plens, gcls, par = take(6)
    own, land = take(4), take(4)
    left, h_qkv, h_pq, h_pp, h_pre, h_slope, h_ffn = take(7)
    if small:
        o_qkv, o_o, o_in, o_out, o_vec, o_gq, o_gp, land_a, land_g, own_g = take(10)
    else:
        vpar, o_gq, o_gp, f_pro, f_att, f_up, f_flo = take(7)
    buffers = take(4)
    bqkv, bo, bin_, bout = buffers
    qkv, pq, pp, source, slope, gsrc = take(6)
    attn_full, attn, steep, flow_full, flow, gmixed, grow = take(7)
    wload, fetch, cload, hsend, hrecv, hlocal, ksem = take(7)
    if small:
        vpar, a_buf, g_buf, stage, s1, r1, s2, r2, s3, r3 = take(10)
        va, ra, vb, rb, vc, rc, rz = take(7)
        s1s, r1s, s2s, r2s, s3s, r3s, vsend, vrecv, zsend, zrecv = take(10)
        gs, gr, ls, lr, sl, gl = take(6)

    core = lax.axis_index("section")
    me = lax.axis_index("batch")
    peer = {"section": 1 - core}
    features = gcls.shape[1]
    total = flow.shape[0]
    split = pq.shape[1]
    count_q, tall = cot_query.shape[0] // 2, cot_passage.shape[0] // 2
    heads_p = pp.shape[0]
    blocks_p = PLEN // QLEN

    def weight_copy(spot, source_set):
        return pltpu.make_async_copy(source_set[spot], buffers[spot], wload.at[spot])

    def weight_start(layer, spot):
        @pl.when(core == layer)
        def _():
            weight_copy(spot, own).start()

        @pl.when(core != layer)
        def _():
            weight_copy(spot, land).start()

    def weight_wait(spot):
        weight_copy(spot, own).wait()

    saved = ((h_ffn, source), (h_slope, slope), (h_pre, source), (h_qkv, qkv), (h_pq, pq), (h_pp, pp))

    def saved_copy(layer, spot):
        src, dst = saved[spot]
        return pltpu.make_async_copy(src.at[layer], dst, fetch.at[spot])

    cots = [
        pltpu.make_async_copy(
            cot_query.at[pl.ds(core * count_q, count_q)], gsrc.at[pl.ds(0, count_q)], cload.at[0]
        ),
        pltpu.make_async_copy(
            cot_passage.at[pl.ds(core * tall, tall)], gsrc.at[pl.ds(count_q, tall)], cload.at[1]
        ),
    ]
    saved_copy(1, 0).start()
    for copy in cots:
        copy.start()
    weight_start(1, 3)
    saved_copy(1, 1).start()

    widths = ((flow, 1), (slope, 4), (attn, 1), (qkv, 3))

    def pieces_of(slot):
        base = (0, 1, 5, 6)[slot]
        ref, count = widths[slot]
        return [(base + item, ref, ref.shape[1] // 2, item) for item in range(count)]

    def own_piece(layer, piece):
        spot, ref, width, item = piece
        lanes = pl.ds(pl.multiple_of(core * width + item * CHUNK, 128), CHUNK)
        return pltpu.make_async_copy(ref.at[:, lanes], own_g.at[layer, spot], ksem.at[spot])

    def peer_piece(layer, piece):
        spot, ref, width, item = piece
        lanes = pl.ds(pl.multiple_of((1 - core) * width + item * CHUNK, 128), CHUNK)
        return remote(
            ref.at[:, lanes], land_g.at[layer, spot], gs.at[layer, spot], gr.at[layer, spot], peer
        )

    def whole_piece(layer, slot):
        ref = widths[slot][0]
        target = (f_flo, f_up, f_att, f_pro)[slot]
        return pltpu.make_async_copy(ref, target.at[layer], ksem.at[slot])

    def give(layer, slot):
        if small:
            for piece in pieces_of(slot):
                peer_piece(layer, piece).start()
                own_piece(layer, piece).start()
        else:
            whole_piece(layer, slot).start()

    def given(layer, slot):
        if small:
            for piece in pieces_of(slot):
                peer_piece(layer, piece).wait_send()
                if slot > 0:
                    own_piece(layer, piece).wait()
                else:

                    @pl.when(layer == 0)
                    def _():
                        own_piece(layer, piece).wait()
        else:
            whole_piece(layer, slot).wait()

    def slot_zero(layer):
        saved_copy(layer, 0).wait()
        gains = par.at[layer]
        last = layer == 1

        def grad_of(index):
            block = gsrc[index].astype(FULL)
            beyond = jnp.maximum(index - count_q, 0)
            item = beyond // blocks_p
            query_limit = qlens[core * count_q + jnp.minimum(index, count_q - 1)]
            passage_limit = (
                plens[core * (tall // blocks_p) + item] - (beyond % blocks_p) * QLEN
            )
            limit = jnp.where(index < count_q, query_limit, passage_limit)
            limit = jnp.where(last, limit, QLEN)
            lead = jnp.where(index < count_q, index, count_q + item)
            starts = (index < count_q) | (beyond % blocks_p == 0)
            row = lax.broadcasted_iota(jnp.int32, block.shape, 0)
            block = jnp.where(row < limit, block, 0.0)
            extra = gcls[pl.ds(lead, 1)] * jnp.where(starts & last, 1.0, 0.0)
            return block + jnp.where(row == 0, extra, 0.0)

        def store(rows, back):
            flow_full[rows] = back
            flow[rows] = back.astype(LOW)

        gain, shift, bias = norm_back(source, grad_of, gains[10:11], total, store)
        sums = vpar.at[layer]
        sums[10:11], sums[11:12], sums[9:10] = gain, shift, bias
        give(layer, 0)
        saved_copy(layer, 2).start()

    width = 256
    tiles = bout.shape[0] // width

    def slot_one(layer):
        saved_copy(layer, 1).wait()
        weight_wait(3)
        sums = vpar.at[layer]

        def shrink(tile):
            rows_of = pl.ds(pl.multiple_of(tile * width, width), width)
            steep[tile % 2] = dot_last(flow[...], bout[rows_of])

        def bend(tile):
            lanes = lane_range(tile, width)
            acc = jnp.zeros((8, width), FULL)
            for index in range(total // ROWS):
                rows = pl.ds(index * ROWS, ROWS)
                low = (steep[tile % 2, rows] * slope[rows, lanes].astype(FULL)).astype(LOW)
                slope[rows, lanes] = low
                acc = acc + add_rows(low.astype(FULL))
            sums[pl.ds(5 + tile // 3, 1), lane_range(tile % 3, width)] = jnp.sum(
                acc, 0, keepdims=True
            )

        shrink(0)

        def both(index):
            shrink(index + 1)
            bend(index)

        over(tiles - 1, both)
        bend(tiles - 1)
        give(layer, 1)

        @pl.when(layer == 1)
        def _():
            weight_start(0, 3)

    def slot_two(layer):
        weight_wait(2)
        flow_full[...] += dot_last(slope[...], bin_[...])
        saved_copy(layer, 2).wait()
        gains, sums = par.at[layer], vpar.at[layer]

        def store(rows, back):
            attn_full[rows] = back
            attn[rows] = back.astype(LOW)

        gain, shift, bias = norm_back(
            source, lambda index: flow_full[row_range(index)], gains[3:4], total, store
        )
        sums[3:4], sums[4:5], sums[2:3] = gain, shift, bias
        give(layer, 2)
        weight_wait(1)
        gmixed[...] = dot_last(attn[...], bo[...]).astype(LOW)

        @pl.when(layer == 1)
        def _():
            weight_start(0, 2)
            weight_start(0, 1)
            saved_copy(0, 0).start()
            saved_copy(0, 1).start()

    blocks = [(0, split, pq, 0)]
    for item in range(heads_p // HEADS):
        blocks.append((split + item * PLEN, PLEN, pp, item * HEADS))

    def attend(index):
        tasks = []
        for step in range(PAIRS):
            for block in blocks:
                tasks.append((index * PAIRS + step,) + block)

        def spot_of(task, offset):
            hp, lo, rows = task[:3]
            return (pl.ds(lo, rows), pl.ds(pl.multiple_of(offset + hp * 128, 128), 128))

        grads = []
        for task in tasks:
            values, back = qkv[spot_of(task, 2 * features)], gmixed[spot_of(task, 0)]
            for head in (0, 1):
                masked = jnp.where(head_lanes(task[2], head), values, LOW(0))
                grads.append(dot_last(masked, back))
        lows = []
        for spot, grad_probs in enumerate(grads):
            hp, lo, rows, probs, base = tasks[spot // 2]
            full = probs[base + 2 * hp + spot % 2].astype(FULL)
            inner = jnp.sum(grad_probs * full, 0, keepdims=True)
            lows.append((full * (grad_probs - inner)).astype(LOW))
        for spot, task in enumerate(tasks):
            hp, lo, rows, probs, base = task
            queries, keys = qkv[spot_of(task, 0)], qkv[spot_of(task, features)]
            back = gmixed[spot_of(task, 0)]
            turned = keys.T
            outs = []
            for head in (0, 1):
                grad_scores = lows[2 * spot + head]
                outs.append(
                    (
                        dot(turned[64 * head : 64 * head + 64], grad_scores) * 0.125,
                        dot(grad_scores, queries) * 0.125,
                        dot(probs[base + 2 * hp + head], back),
                    )
                )
            first = head_lanes(rows, 0)
            both = jnp.concatenate([outs[0][0], outs[1][0]], 0)
            qkv[spot_of(task, 0)] = both.astype(LOW).T
            for item in (1, 2):
                both = jnp.where(first, outs[0][item], outs[1][item])
                qkv[spot_of(task, item * features)] = both.astype(LOW)

    def grads_here(spot):
        lo, count, target = ((0, count_q, o_gq), (count_q, tall, o_gp))[spot]
        return pltpu.make_async_copy(
            grow.at[pl.ds(lo, count)], target.at[pl.ds(core * count, count)], hlocal.at[spot]
        )

    def grads_there(spot):
        lo, count, target = ((0, count_q, o_gq), (count_q, tall, o_gp))[spot]
        return remote(
            grow.at[pl.ds(lo, count)],
            target.at[pl.ds(core * count, count)],
            hsend.at[spot],
            hrecv.at[spot],
            peer,
        )

    def slot_three(layer):
        for spot in (3, 4, 5):
            saved_copy(layer, spot).wait()
        over(features // 128 // PAIRS, attend)
        give(layer, 3)
        sums = vpar.at[layer]

        def bias_sums(index, carry):
            rows = row_range(index)
            return (
                carry[0] + add_rows(qkv[rows, pl.ds(0, features)].astype(FULL)),
                carry[1] + add_rows(qkv[rows, pl.ds(2 * features, features)].astype(FULL)),
            )

        zero = jnp.zeros((8, features), FULL)
        found = lax.fori_loop(0, total // ROWS, bias_sums, (zero, zero), unroll=2)
        sums[0:1] = jnp.sum(found[0], 0, keepdims=True)
        sums[1:2] = jnp.sum(found[1], 0, keepdims=True)
        sums[12:16] = jnp.zeros((4, features), FULL)
        weight_wait(0)
        rows_all = attn_full[...] + dot_last(qkv[...], bqkv[...])
        grow[...] = rows_all.reshape(grow.shape)
        gsrc[...] = rows_all.astype(LOW).reshape(gsrc.shape)

        @pl.when(core == layer)
        def _():
            for spot in (0, 1):
                grads_here(spot).start()

        @pl.when(core != layer)
        def _():
            for spot in (0, 1):
                grads_there(spot).start()

        @pl.when(layer == 1)
        def _():
            weight_start(0, 0)

    def grads_given(layer):
        @pl.when(core == layer)
        def _():
            for spot in (0, 1):
                grads_here(spot).wait()

        @pl.when(core != layer)
        def _():
            for spot in (0, 1):
                grads_there(spot).wait_send()

    slots = (slot_zero, slot_one, slot_two, slot_three)

    def reload(layer, slot):
        @pl.when(layer == 1)
        def _():
            if slot == 3:
                for spot in (3, 4, 5):
                    saved_copy(0, spot).start()

    def rest_of_loads():
        for spot in (2, 1, 0):
            weight_start(1, spot)
        for spot in (3, 4, 5):
            saved_copy(1, spot).start()

    def grads_came():
        lands = ((o_gq, count_q), (o_gp, tall))
        for spot, (target, count) in enumerate(lands):
            there = target.at[pl.ds((1 - core) * count, count)]
            remote(there, there, hsend.at[spot], hrecv.at[spot], peer).wait_recv()

    if not small:
        greet([peer])
        rest_of_loads()
        for copy in cots:
            copy.wait()
        for layer in (1, 0):
            for slot in range(4):
                slots[slot](layer)
                given(layer, slot)
                reload(layer, slot)
            grads_given(layer)
        grads_came()
        return

    x, y, z = me % 2, (me // 2) % 2, me // 4
    px, py = me + 1 - 2 * x, me + 2 - 4 * y
    targets = [{"batch": px}, {"batch": py}, peer]
    for step in (1, 2, 3):
        other = ((z + step) % 4) * 4 + me % 4
        targets += [{"section": sec, "batch": other} for sec in (0, 1)]
    greet(targets)

    def left_there(layer, spot):
        return remote(
            left.at[layer, spot], land_a.at[layer, spot], ls.at[layer, spot], lr.at[layer, spot],
            peer,
        )

    def stage_copy(number, side):
        layer, spot = 1 - number // 7, number % 7
        src = left if side == 0 else land_a
        return pltpu.make_async_copy(
            src.at[layer, spot], stage.at[number % 2, side], sl.at[number % 2, side]
        )

    def stage_start(number):
        stage_copy(number, 0).start()
        left_there(1 - number // 7, number % 7).wait_recv()
        stage_copy(number, 1).start()

    def turn(number, spot):
        for side in (0, 1):
            stage_copy(number, side).wait()
        for side in (0, 1):
            lanes = pl.ds(side * total, total)
            for half in range(features // CHUNK):
                block = stage[number % 2, side, :, pl.ds(half * CHUNK, CHUNK)].T
                if spot > 3:
                    a_buf[spot, pl.ds(2 * half, 2), :, :, :, lanes] = block.reshape(
                        2, 2, 2, BLOCK, total
                    )
                else:
                    shaped = block.reshape(2, 4, BLOCK, total)
                    for item in range(4):
                        a_buf[item, spot, half, :, :, lanes] = shaped[:, item]

        @pl.when(number + 2 < 14)
        def _():
            stage_start(number + 2)

    def right_copy(layer, spot, side):
        src = own_g if side == 0 else land_g
        return pltpu.make_async_copy(
            src.at[layer, spot], g_buf.at[spot, pl.ds(side * total, total)], gl.at[spot, side]
        )

    def right_start(k):
        ch = k % COUNT
        layer = 1 - k // COUNT

        @pl.when((k < 2 * COUNT) & ((ch == 0) | (ch >= 4)))
        def _():
            spot = right_index(ch)
            right_copy(layer, spot, 0).start()
            remote(
                own_g.at[layer, spot], land_g.at[layer, spot],
                gs.at[layer, spot], gr.at[layer, spot], peer,
            ).wait_recv()
            right_copy(layer, spot, 1).start()

    RING = 12

    def first(k, par_):
        return remote(
            s1.at[k % 4], r1.at[k % RING], s1s.at[k], r1s.at[k],
            {"batch": px if par_ == 0 else py},
        )

    def second(k, par_):
        return remote(
            s2.at[k % 4], r2.at[k % RING], s2s.at[k], r2s.at[k],
            {"batch": py if par_ == 0 else px},
        )

    def third(k, step):
        layer = 1 - k // COUNT
        zt = (z + step) % 4
        return remote(
            s3.at[k % 4, zt], r3.at[core, k % COUNT, z], s3s.at[k, step],
            r3s.at[core, k % COUNT, z], {"section": layer, "batch": zt * 4 + me % 4},
        )

    def third_in(k, step, src_core):
        zs = (z + 4 - step) % 4
        return remote(
            s3.at[k % 4, zs], r3.at[src_core, k % COUNT, zs], s3s.at[k, step],
            r3s.at[src_core, k % COUNT, zs], peer,
        )

    def product(k, block, rows):
        return dot(block.reshape(rows, 2 * total), g_buf[right_index(k % COUNT)])

    def left_of(k):
        return a_buf.at[left_index(k % COUNT)]

    def ready(k, par_):
        ch = k % COUNT

        @pl.when((ch == 0) | (ch >= 4))
        def _():
            for side in (0, 1):
                right_copy(0, right_index(ch), side).wait()

        base = (k // COUNT) * 7
        if par_ == 0:

            @pl.when(ch == 0)
            def _():
                for spot in range(4):
                    turn(base + spot, spot)

            for spot, at in ((4, 4), (5, 8)):

                @pl.when(ch == at)
                def _():
                    turn(base + spot, spot)
        else:

            @pl.when(ch == 9)
            def _():
                turn(base + 6, 6)

    def part_one(k, par_):
        ready(k, par_)
        ref = left_of(k)
        block = ref[:, :, 1 - x] if par_ == 0 else ref[:, 1 - y]
        s1[k % 4] = product(k, block, 8 * BLOCK).astype(LOW).reshape(4, 2, BLOCK, CHUNK)
        first(k, par_).start()

    def part_two(k, par_):
        first(k, par_).wait()
        ref = left_of(k)
        if par_ == 0:
            block, came = ref[:, 1 - y, x], r1[k % RING, :, 1 - y]
        else:
            block, came = ref[:, y, 1 - x], r1[k % RING, :, 1 - x]
        value = product(k, block, 4 * BLOCK).reshape(4, BLOCK, CHUNK) + came.astype(FULL)
        s2[k % 4] = value.astype(LOW)
        second(k, par_).start()

    def part_three(k, par_):
        second(k, par_).wait()
        layer = 1 - k // COUNT
        ref = left_of(k)
        came = r1[k % RING, :, y] if par_ == 0 else r1[k % RING, :, x]
        value = (
            product(k, ref[:, y, x], 4 * BLOCK).reshape(4, BLOCK, CHUNK)
            + came.astype(FULL)
            + r2[k % RING].astype(FULL)
        )
        s3[k % 4] = value.astype(LOW)
        for step in (1, 2, 3):
            third(k, step).start()

        @pl.when(core != layer)
        def _():
            third(k, 0).start()

        @pl.when(core == layer)
        def _():
            r3[core, k % COUNT, z] = s3[k % 4, z]

    def part_four(k):
        layer = 1 - k // COUNT
        ch = k % COUNT
        for step in (1, 2, 3):
            third(k, step).wait_send()

        @pl.when(core != layer)
        def _():
            third(k, 0).wait_send()

        @pl.when(core == layer)
        def _():
            for step in (1, 2, 3):
                for src_core in (0, 1):
                    third_in(k, step, src_core).wait_recv()
            third_in(k, 0, 1 - core).wait_recv()
            for src_core in (0, 1):
                value = jnp.sum(r3[src_core, ch].astype(FULL), 0)

                @pl.when(ch < 4)
                def _():
                    o_out[ch, :, pl.ds(src_core * CHUNK, CHUNK)] = value

                @pl.when((ch >= 4) & (ch < 8))
                def _():
                    start = pl.multiple_of((ch - 4) * CHUNK + src_core * 4 * CHUNK, 128)
                    o_in[:, pl.ds(start, CHUNK)] = value

                @pl.when(ch == 8)
                def _():
                    o_o[:, pl.ds(src_core * CHUNK, CHUNK)] = value

                @pl.when(ch >= 9)
                def _():
                    start = pl.multiple_of((ch - 9) * CHUNK + src_core * 3 * CHUNK, 128)
                    o_qkv[:, pl.ds(start, CHUNK)] = value

    vec_cross = remote(vpar.at[1 - core], ra, vsend.at[0], vrecv.at[0], peer)
    vec_x = remote(va, rb, vsend.at[1], vrecv.at[1], {"batch": px})
    vec_y = remote(vb, rc, vsend.at[2], vrecv.at[2], {"batch": py})

    def vec_z(step, slot):
        return remote(
            vc, rz.at[slot], zsend.at[step], zrecv.at[slot],
            {"batch": ((z + step) % 4) * 4 + me % 4},
        )

    steps = 2 * COUNT + 6

    def pair(turn_index, carry):
        kk = turn_index - 1
        layer = (kk < 3).astype(jnp.int32)

        for slot, (one, two) in enumerate(((0, 4), (1, 4), (2, 5), (3, 6))):

            @pl.when((kk == one) | (kk == two))
            def _():
                done = (kk == one).astype(jnp.int32)
                given(done, slot)
                reload(done, slot)
                if slot == 3:
                    grads_given(done)

        @pl.when(kk == 0)
        def _():
            for spot in (4, 5, 6):
                left_there(1, spot).start()

        @pl.when(kk == 2)
        def _():
            for spot in range(7):
                left_there(0, spot).start()

        @pl.when(kk == -1)
        def _():
            for spot in range(4):
                left_there(1, spot).start()
            rest_of_loads()
            for copy in cots:
                copy.wait()

        for par_ in (0, 1):
            k = 2 * kk + par_

            @pl.when((k >= 0) & (k < 2 * COUNT))
            def _():
                part_one(k, par_)

        for par_ in (0, 1):
            k = 2 * kk + par_

            @pl.when((k >= 2) & (k < 2 * COUNT + 2))
            def _():
                part_two(k - 2, par_)

            @pl.when((k >= 4) & (k < 2 * COUNT + 4))
            def _():
                part_three(k - 4, par_)

            @pl.when(k >= 6)
            def _():
                part_four(k - 6)

        for slot, (one, two) in enumerate(((-1, 3), (0, 3), (1, 4), (2, 5))):

            @pl.when((kk == one) | (kk == two))
            def _():
                slots[slot](layer)

        @pl.when(kk == -1)
        def _():
            stage_start(0)
            stage_start(1)
            own_piece(1, pieces_of(0)[0]).wait()

        @pl.when((kk >= -1) & (kk < COUNT - 1))
        def _():
            for par_ in (0, 1):
                right_start(2 * kk + 2 + par_)

        @pl.when(kk == 6)
        def _():
            vec_cross.start()

        @pl.when(kk == 7)
        def _():
            vec_cross.wait()
            va[...] = vpar[core] + ra[...]
            vec_x.start()

        @pl.when(kk == 8)
        def _():
            vec_x.wait()
            vb[...] = va[...] + rb[...]
            vec_y.start()

        @pl.when(kk == 9)
        def _():
            vec_y.wait()
            vc[...] = vb[...] + rc[...]
            for step in (1, 2, 3):
                vec_z(step, z).start()

        @pl.when(kk == 11)
        def _():
            for step in (1, 2, 3):
                vec_z(step, z).wait_send()
                vec_z(step, (z + 4 - step) % 4).wait_recv()
            rz[z] = vc[...]
            o_vec[...] = jnp.sum(rz[...], 0)

        return carry

    lax.fori_loop(0, steps // 2 + 1, pair, 0)
    grads_came()
    for layer in (0, 1):
        for spot in range(7):
            left_there(layer, spot).wait_send()


def backward_both(parts, cots, qlens, plens, gcls, par, own, land, kept):
    small = parts == 16
    cot_query, cot_passage = cots
    left, h_qkv, h_pq, h_pp, h_pre, h_slope, h_ffn = kept
    total, features = left.shape[2:]
    wide = own[2].shape[1]
    shape = jax.ShapeDtypeStruct
    anywhere = pl.BlockSpec(memory_space=pl.ANY)
    vmem = pl.BlockSpec(memory_space=pltpu.VMEM)
    smem = pl.BlockSpec(memory_space=pltpu.SMEM)
    dma = pltpu.SemaphoreType.DMA
    grads = [shape(cot_query.shape, FULL), shape(cot_passage.shape, FULL)]
    if small:
        out_shape = [
            shape((BLOCK, 3 * features), FULL),
            shape((BLOCK, features), FULL),
            shape((BLOCK, wide), FULL),
            shape((4, BLOCK, features), FULL),
            shape((16, features), FULL),
            *grads,
            shape((2, 7, total, features), LOW),
            shape((2, 9, total, CHUNK), LOW),
            shape((2, 9, total, CHUNK), LOW),
        ]
        out_specs = [vmem] * 5 + [anywhere] * 5
    else:
        out_shape = [
            shape((2, 16, features), FULL),
            *grads,
            shape((2, total, 3 * features), LOW),
            shape((2, total, features), LOW),
            shape((2, total, wide), LOW),
            shape((2, total, features), LOW),
        ]
        out_specs = [vmem] + [anywhere] * 6
    scratch = [pltpu.VMEM(item.shape, item.dtype) for item in own]
    scratch += [
        pltpu.VMEM(h_qkv.shape[1:], LOW),
        pltpu.VMEM(h_pq.shape[1:], LOW),
        pltpu.VMEM(h_pp.shape[1:], LOW),
        pltpu.VMEM((total, features), FULL),
        pltpu.VMEM((total, wide), LOW),
        pltpu.VMEM((total // QLEN, QLEN, features), LOW),
        pltpu.VMEM((total, features), FULL),
        pltpu.VMEM((total, features), LOW),
        pltpu.VMEM((2, total, 256), FULL),
        pltpu.VMEM((total, features), FULL),
        pltpu.VMEM((total, features), LOW),
        pltpu.VMEM((total, features), LOW),
        pltpu.VMEM((total // QLEN, QLEN, features), FULL),
        dma((4,)),
        dma((6,)),
        dma((2,)),
        dma((2,)),
        dma((2,)),
        dma((2,)),
        dma((9,)),
    ]
    if small:
        steps = 2 * COUNT
        vector = pltpu.VMEM((16, features), FULL)
        scratch += [
            pltpu.VMEM((2, 16, features), FULL),
            pltpu.VMEM((7, 4, 2, 2, BLOCK, 2 * total), LOW),
            pltpu.VMEM((9, 2 * total, CHUNK), LOW),
            pltpu.VMEM((2, 2, total, features), LOW),
            pltpu.VMEM((4, 4, 2, BLOCK, CHUNK), LOW),
            pltpu.VMEM((12, 4, 2, BLOCK, CHUNK), LOW),
            pltpu.VMEM((4, 4, BLOCK, CHUNK), LOW),
            pltpu.VMEM((12, 4, BLOCK, CHUNK), LOW),
            pltpu.VMEM((4, 4, BLOCK, CHUNK), LOW),
            pltpu.VMEM((2, COUNT, 4, BLOCK, CHUNK), LOW),
            *[vector] * 6,
            pltpu.VMEM((4, 16, features), FULL),
            dma((steps,)),
            dma((steps,)),
            dma((steps,)),
            dma((steps,)),
            dma((steps, 4)),
            dma((2, COUNT, 4)),
            dma((3,)),
            dma((3,)),
            dma((4,)),
            dma((4,)),
            dma((2, 9)),
            dma((2, 9)),
            dma((2, 7)),
            dma((2, 7)),
            dma((2, 2)),
            dma((9, 2)),
        ]
    return pl.pallas_call(
        functools.partial(backward_kernel, parts),
        out_shape=out_shape,
        in_specs=[anywhere, anywhere, smem, smem, vmem, vmem] + [anywhere] * 15,
        out_specs=out_specs,
        scratch_shapes=scratch,
        compiler_params=pltpu.CompilerParams(
            collective_id=1, has_side_effects=True, vmem_limit_bytes=60 * 1024 * 1024
        ),
    )(cot_query, cot_passage, qlens, plens, gcls, par, *own, *land, *kept)


def per_device(
    parts,
    x_query,
    x_passage,
    len_query,
    len_passage,
    positive,
    cot_query,
    cot_passage,
    *weights,
):
    core = lax.axis_index("section")
    on_first = core == 0
    own_set = [member[0] for member in weights]
    own = [own_set[item] for item in (0, 2, 6, 8)]
    vectors = [weights[item] for item in (1, 3, 4, 5, 7, 9, 10, 11)]
    features = x_query.shape[2]
    half_q, half_p = x_query.shape[0] // 2, x_passage.shape[0] // 2
    *kept, par, l_qkv, l_o, l_in, l_out, hidden_q, hidden_p, grad_cls, loss = forward_both(
        parts,
        x_query,
        x_passage.reshape(-1, QLEN, features),
        len_query,
        len_passage,
        positive,
        vectors,
        own,
    )
    other = (l_qkv, l_o, l_in, l_out)
    hidden_q, hidden_p = hidden_q[None], hidden_p.reshape(x_passage.shape)[None]
    if parts == 16:
        loss_value = loss[0, 0]
    else:
        targets = lax.all_gather(positive, "batch", axis=0, tiled=True)
        own_q = hidden_q[0, :, 0]
        own_p = hidden_p[0, :, 0]
        last_q, last_p = (jnp.where(on_first, swap(item), item) for item in (own_q, own_p))
        cls_query = lax.all_gather(last_q, "batch", axis=0, tiled=True)
        cls_passage = lax.all_gather(last_p, "batch", axis=0, tiled=True)
        score_scale = 2.0 / math.sqrt(features)
        logits = (
            jnp.einsum("qd,pd->qp", cls_query, cls_passage, preferred_element_type=jnp.float32)
            * score_scale
        )
        term_values, grad_logits = contrast(logits, targets)
        loss_value = jnp.mean(term_values)
        mine = lax.axis_index("batch") * 2 + core
        own_logits = lax.dynamic_slice_in_dim(grad_logits, mine * half_q, half_q, 0)
        grad_cls_q = (
            jnp.einsum("qp,pd->qd", own_logits, cls_passage, preferred_element_type=jnp.float32)
            * score_scale
        )
        own_columns = lax.dynamic_slice_in_dim(grad_logits, mine * half_p, half_p, 1)
        grad_cls_p = (
            jnp.einsum("qp,qd->pd", own_columns, cls_query, preferred_element_type=jnp.float32)
            * score_scale
        )
        grad_cls = jnp.concatenate([grad_cls_q, grad_cls_p], 0)
        grad_cls = jnp.pad(grad_cls, ((0, 8 - grad_cls.shape[0]), (0, 0)))

    outs = backward_both(
        parts,
        (cot_query, cot_passage.reshape(-1, QLEN, features)),
        len_query,
        len_passage,
        grad_cls,
        par,
        own,
        other,
        kept,
    )
    groups = ((0, 2), (2, 1), (3, 1), (4, 1), (5, 4), (9, 1), (10, 1), (11, 1))
    if parts == 16:
        d_qkv, d_o, d_in, d_out, d_vec, grad_q, grad_p = outs[:7]
        d_out = d_out.reshape(-1, features)
        batch = lax.axis_index("batch")
        small = []
        for at, count in groups:
            flat = d_vec[at : at + count].reshape(-1)
            size = flat.shape[0] // parts
            small.append(lax.dynamic_slice_in_dim(flat, batch * size, size, 0))
    else:
        sums, grad_q, grad_p, g_pro, g_att, g_up, g_flo = outs
        left = kept[0]

        def total(pair):
            kept_one = jnp.where(on_first, pair[0], pair[1])
            both = kept_one + swap(jnp.where(on_first, pair[1], pair[0]))
            return lax.psum_scatter(both, "batch", scatter_dimension=0, tiled=True)

        def product(first, second):
            return jnp.einsum("rd,re->de", first, second, preferred_element_type=jnp.float32)

        d_qkv, d_o, d_in = (
            total([product(left[layer, spot], right[layer]) for layer in (0, 1)])
            for spot, right in ((6, g_pro), (5, g_att), (4, g_up))
        )
        d_out = total(
            [
                jnp.concatenate([product(left[layer, spot], g_flo[layer]) for spot in range(4)], 0)
                for layer in (0, 1)
            ]
        )
        small = [
            total([sums[layer, at : at + count].reshape(-1) for layer in (0, 1)])
            for at, count in groups
        ]
    grad_q = grad_q[None]
    grad_p = grad_p.reshape(x_passage.shape)[None]
    d_b_qv, d_b_o, d_g_attn, d_c_attn, d_b_in, d_b_out, d_g_ffn, d_c_ffn = small
    outs = (
        d_qkv, d_b_qv, d_o, d_b_o, d_g_attn, d_c_attn, d_in, d_b_in, d_out, d_b_out, d_g_ffn,
        d_c_ffn,
    )
    return (hidden_q, hidden_p, grad_q, grad_p, loss_value) + tuple(item[None] for item in outs)


def solution(mesh):
    in_specs = (
        P("batch", None, None),
        P("batch", None, None),
        P("batch"),
        P("batch"),
        P("batch"),
        P("batch", None, None),
        P("batch", None, None),
        P("section", None, None),
        P("section", None),
        P("section", None, None),
        P("section", None),
        P("section", None),
        P("section", None),
        P("section", None, None),
        P("section", None),
        P("section", None, None),
        P("section", None),
        P("section", None),
        P("section", None),
    )
    out_specs = (
        P("section", "batch", None, None),
        P("section", "batch", None, None),
        P("section", "batch", None, None),
        P("section", "batch", None, None),
        P(),
        P("section", "batch", None),
        P("section", "batch"),
        P("section", "batch", None),
        P("section", "batch"),
        P("section", "batch"),
        P("section", "batch"),
        P("section", "batch", None),
        P("section", "batch"),
        P("section", "batch", None),
        P("section", "batch"),
        P("section", "batch"),
        P("section", "batch"),
    )
    return jax.shard_map(
        functools.partial(per_device, mesh.shape["batch"]), mesh=mesh, in_specs=in_specs, out_specs=out_specs, check_vma=False
    )
```

profile of v0, /device:TPU:0, one launch (start us, length us, event | category | flops | bytes accessed | tf_op | source)
XLA Modules:
  0.0 231.2 jit_solution(2231398846531641224)
XLA Ops:
  0.7 55.3 %shard_map.314 = (bf16[2,7,384,768]{3,2,1,0:T(8,128)(2,1)}, bf16[2,384,2304]{2,1,0:T(8,128)(2,1)}, bf16[2,12,128,128]{3,2,1,0:T(8,128)(2,1)}, bf16[2,12,256,256]...) custom-call(bf16[8,32,768]{2,1,0:T(8,128)(2,1)} %x_query.1, ...), custom_call_target="tpu_custom_call" | custom-call | tf_op jit(solution)/shard_map/pallas_call | solution.py:541
  56.0 1.2 slice.27
  57.2 160.5 %shard_map.315 = (f32[48,2304]{1,0:T(8,128)}, f32[48,768]{1,0:T(8,128)}, f32[48,3072]{1,0:T(8,128)}, f32[4,48,768]{2,1,0:T(8,128)}, f32[16,768]{1,0:T(8,128)}, /...) custom-call(bf16[8,32,768]{2,1,0:T(8,128)(2,1)} %refs_0_.1, ...), custom_call_target="tpu_custom_call" | custom-call | tf_op jit(solution)/shard_map/pallas_call | solution.py:1379
  217.7 0.0 copy-start
  217.7 0.9 slice.28
  218.6 0.6 dynamic-slice_bitcast_fusion
  219.2 0.8 slice.32
  220.0 0.9 fusion
  220.8 0.6 constant_dynamic-slice_fusion
  221.4 0.6 dynamic_slice.28
  222.1 0.6 constant_dynamic-slice_fusion.2
  222.7 0.6 constant_dynamic-slice_fusion.4
  223.3 0.0 copy-done.5
  223.3 0.7 copy.44
  224.0 0.0 copy-done.1
  224.0 0.9 copy.45
  224.9 2.1 copy.46
  227.0 0.0 copy-done
  227.0 1.1 copy.47
  228.2 0.8 copy.48
  228.9 0.7 copy.49
  229.6 0.0 copy-done.3
  229.6 0.8 copy.50
  230.4 0.8 copy.51
  (11 shorter events, 0.0 us)
Async XLA Ops:
  57.2 166.1 %copy-start.5 = (bf16[8,32,768]{2,1,0:T(8,128)(2,1)S(1)}, bf16[8,32,768]{2,1,0:T(8,128)(2,1)}, u32[]{:S(2)}) copy-start(bf16[8,32,768]{2,1,0:T(8,128)(2,1)} %get-tuple-element.40) | copy-start | bytes 1179652
  57.2 166.8 %copy-start.1 = (bf16[16,32,768]{2,1,0:T(8,128)(2,1)S(1)}, bf16[16,32,768]{2,1,0:T(8,128)(2,1)}, u32[]{:S(2)}) copy-start(bf16[16,32,768]{2,1,0:T(8,128)(2,1)} %get-tuple-element.41) | copy-start | bytes 2359300
  217.7 9.3 %copy-start = (f32[16,32,768]{2,1,0:T(8,128)S(1)}, f32[16,32,768]{2,1,0:T(8,128)}, u32[]{:S(2)}) copy-start(f32[16,32,768]{2,1,0:T(8,128)} %get-tuple-element.56) | copy-start | bytes 4718596
  223.3 4.9 %copy-start.4 = (f32[48,2304]{1,0:T(8,128)S(1)}, f32[48,2304]{1,0:T(8,128)}, u32[]{:S(2)}) copy-start(f32[48,2304]{1,0:T(8,128)} %get-tuple-element.58) | copy-start | bytes 1327108
  224.0 4.9 %copy-start.6 = (f32[48,768]{1,0:T(8,128)S(1)}, f32[48,768]{1,0:T(8,128)}, u32[]{:S(2)}) copy-start(f32[48,768]{1,0:T(8,128)} %get-tuple-element.60) | copy-start | bytes 442372
  224.0 5.6 %copy-start.3 = (f32[48,3072]{1,0:T(8,128)S(1)}, f32[48,3072]{1,0:T(8,128)}, u32[]{:S(2)}) copy-start(f32[48,3072]{1,0:T(8,128)} %get-tuple-element.61) | copy-start | bytes 1769476
  224.9 5.5 %copy-start.2 = (f32[4,48,768]{2,1,0:T(8,128)S(1)}, f32[4,48,768]{2,1,0:T(8,128)}, u32[]{:S(2)}) copy-start(f32[4,48,768]{2,1,0:T(8,128)} %get-tuple-element.62) | copy-start | bytes 1769476
where the time goes:
time: 232 us; the launch traced here: 231 us
  Pallas kernels  216 us (93%)
  local copies, waits for them, and re-layouts  14.7 us (6%)
    pallas_call x1, Pallas kernels, backward_both(): pl.pallas_call(functools.partial(backward_kernel, parts), out_shape=out_s...  160 us
    pallas_call x1, Pallas kernels, forward_both(): pl.pallas_call(functools.partial(forward_kernel, parts), out_shape=[shape...  55.3 us
    unnamed x22, local copies, waits for them, and re-layouts  7.98 us

commit v1 on v0

--- a/solution.py
+++ b/solution.py
@@ -132,10 +132,10 @@
     parts, x_query, x_passage, qlens, plens, positive,
     b_qv, b_o, g_attn, c_attn, b_in, b_out, g_ffn, c_ffn, wqkv, wo, win, wout,
     o_left, o_qkv, o_pq, o_pp, o_pre, o_slope, o_ffn, both_par,
-    l_qkv, l_o, l_in, l_out, hid_q, hid_p, gcls, loss,
+    l_qkv, l_o, l_in, l_out, hid_q, hid_p, land_a, gcls, loss,
     tok, out, bqkv, bo, bin_, bout, qkv, pq, pp, mixed, pre, normed_full, normed, up, act,
     slope, ffn, rows8, rows48, packed, every, stack,
-    load, save, xload, parsend, parrecv, wsend, wrecv, hsend, hrecv, hlocal, gsend, grecv, psend, precv,
+    load, save, xload, parsend, parrecv, wsend, wrecv, hsend, hrecv, hlocal, gsend, grecv, psend, precv, asend, arecv,
 ):
     core = lax.axis_index("section")
     me = lax.axis_index("batch")
@@ -238,6 +238,18 @@
         )
         saves[name, layer].start()
 
+    places = {"act0": 0, "act1": 1, "act2": 2, "act3": 3, "normed": 4, "mixed": 5, "tok": 6}
+
+    def left_give(layer, spot, source):
+        return remote(
+            source, land_a.at[layer, spot], asend.at[layer, spot], arecv.at[layer, spot], peer
+        )
+
+    def keep_left(name, layer, source):
+        keep(name, layer, source, o_left.at[layer, places[name]])
+        if layer == 1:
+            left_give(1, places[name], source).start()
+
     def free(name, layer):
         if layer == 1:
             saves[name, 0].wait()
@@ -256,7 +268,7 @@
         base_row = 0
         par = both_par.at[layer]
         x = tok.at[layer].reshape(total, features)
-        keep("tok", layer, x, o_left.at[layer, 6])
+        keep_left("tok", layer, x)
         weight(layer, 0)
         free("qkv", layer)
 
@@ -270,7 +282,10 @@
         keep("qkv", layer, qkv, o_qkv.at[layer])
         if layer == 1:
             fetch_second(3)
-        for name in ("pq", "pp", "mixed"):
+            for name, spot in places.items():
+                saves[name, 0].wait()
+                left_give(0, spot, o_left.at[0, spot]).start()
+        for name in ("pq", "pp"):
             free(name, layer)
 
         def attend(index):
@@ -311,7 +326,7 @@
         over(features // 128 // PAIRS, attend)
         keep("pq", layer, pq, o_pq.at[layer])
         keep("pp", layer, pp, o_pp.at[layer])
-        keep("mixed", layer, mixed, o_left.at[layer, 5])
+        keep_left("mixed", layer, mixed)
         weight(layer, 1)
         free("pre", layer)
         pre[...] = (
@@ -321,7 +336,6 @@
         if layer == 0:
             fetch_second(0)
             fetch_second(1)
-        free("normed", layer)
 
         def norm_one(index):
             rows = row_range(index)
@@ -331,10 +345,8 @@
             normed[rows] = block.astype(LOW)
 
         over(total // ROWS, norm_one, UNROLL)
-        keep("normed", layer, normed, o_left.at[layer, 4])
+        keep_left("normed", layer, normed)
         weight(layer, 2)
-        for item in range(4):
-            free("act%d" % item, layer)
         free("slope", layer)
         step_width = 256
         tiles = win.shape[1] // step_width
@@ -365,7 +377,7 @@
         bend(tiles - 1)
         for item in range(4):
             lanes = pl.ds(item * features, features)
-            keep("act%d" % item, layer, act.at[:, lanes], o_left.at[layer, item])
+            keep_left("act%d" % item, layer, act.at[:, lanes])
         keep("slope", layer, slope, o_slope.at[layer])
         weight(layer, 3)
         free("ffn", layer)
@@ -476,7 +488,9 @@
     for (name, layer), copy in saves.items():
         if layer == 1:
             copy.wait()
-    saves["tok", 0].wait()
+    for layer in (0, 1):
+        for spot in range(7):
+            left_give(layer, spot, o_left.at[layer, spot]).wait()
 
 
 def forward_both(parts, x_query, x_passage, qlens, plens, positive, vectors, own):
@@ -537,6 +551,8 @@
         dma((16,)),
         dma,
         dma,
+        dma((2, 7)),
+        dma((2, 7)),
     ]
     return pl.pallas_call(
         functools.partial(forward_kernel, parts),
@@ -545,11 +561,12 @@
         + [
             shape(x_query.shape, LOW),
             shape(x_passage.shape, LOW),
+            shape((2, 7, total, features), LOW),
             shape((8, features), FULL),
             shape((8, 128), FULL),
         ],
         in_specs=[anywhere, anywhere, smem, smem, smem] + [vmem] * 8 + [anywhere] * 4,
-        out_specs=[anywhere] * 7 + [vmem] + [anywhere] * 6 + [vmem] * 2,
+        out_specs=[anywhere] * 7 + [vmem] + [anywhere] * 7 + [vmem] * 2,
         scratch_shapes=scratch,
         compiler_params=pltpu.CompilerParams(
             collective_id=2, has_side_effects=True, vmem_limit_bytes=VMEM_LIMIT
@@ -607,9 +624,9 @@
 
     cot_query, cot_passage, qlens, plens, gcls, par = take(6)
     own, land = take(4), take(4)
-    left, h_qkv, h_pq, h_pp, h_pre, h_slope, h_ffn = take(7)
+    left, h_qkv, h_pq, h_pp, h_pre, h_slope, h_ffn, land_a = take(8)
     if small:
-        o_qkv, o_o, o_in, o_out, o_vec, o_gq, o_gp, land_a, land_g, own_g = take(10)
+        o_qkv, o_o, o_in, o_out, o_vec, o_gq, o_gp, land_g, own_g = take(9)
     else:
         vpar, o_gq, o_gp, f_pro, f_att, f_up, f_flo = take(7)
     buffers = take(4)
@@ -621,7 +638,7 @@
         vpar, a_buf, g_buf, stage, s1, r1, s2, r2, s3, r3 = take(10)
         va, ra, vb, rb, vc, rc, rz = take(7)
         s1s, r1s, s2s, r2s, s3s, r3s, vsend, vrecv, zsend, zrecv = take(10)
-        gs, gr, ls, lr, sl, gl = take(6)
+        gs, gr, sl, gl = take(4)
 
     core = lax.axis_index("section")
     me = lax.axis_index("batch")
@@ -965,12 +982,6 @@
         targets += [{"section": sec, "batch": other} for sec in (0, 1)]
     greet(targets)
 
-    def left_there(layer, spot):
-        return remote(
-            left.at[layer, spot], land_a.at[layer, spot], ls.at[layer, spot], lr.at[layer, spot],
-            peer,
-        )
-
     def stage_copy(number, side):
         layer, spot = 1 - number // 7, number % 7
         src = left if side == 0 else land_a
@@ -980,7 +991,6 @@
 
     def stage_start(number):
         stage_copy(number, 0).start()
-        left_there(1 - number // 7, number % 7).wait_recv()
         stage_copy(number, 1).start()
 
     def turn(number, spot):
@@ -1188,20 +1198,10 @@
                 if slot == 3:
                     grads_given(done)
 
-        @pl.when(kk == 0)
-        def _():
-            for spot in (4, 5, 6):
-                left_there(1, spot).start()
-
-        @pl.when(kk == 2)
-        def _():
-            for spot in range(7):
-                left_there(0, spot).start()
-
         @pl.when(kk == -1)
         def _():
-            for spot in range(4):
-                left_there(1, spot).start()
+            stage_start(0)
+            stage_start(1)
             rest_of_loads()
             for copy in cots:
                 copy.wait()
@@ -1236,8 +1236,6 @@
 
         @pl.when(kk == -1)
         def _():
-            stage_start(0)
-            stage_start(1)
             own_piece(1, pieces_of(0)[0]).wait()
 
         @pl.when((kk >= -1) & (kk < COUNT - 1))
@@ -1280,15 +1278,12 @@
 
     lax.fori_loop(0, steps // 2 + 1, pair, 0)
     grads_came()
-    for layer in (0, 1):
-        for spot in range(7):
-            left_there(layer, spot).wait_send()
 
 
 def backward_both(parts, cots, qlens, plens, gcls, par, own, land, kept):
     small = parts == 16
     cot_query, cot_passage = cots
-    left, h_qkv, h_pq, h_pp, h_pre, h_slope, h_ffn = kept
+    left, h_qkv, h_pq, h_pp, h_pre, h_slope, h_ffn = kept[:7]
     total, features = left.shape[2:]
     wide = own[2].shape[1]
     shape = jax.ShapeDtypeStruct
@@ -1305,11 +1300,10 @@
             shape((4, BLOCK, features), FULL),
             shape((16, features), FULL),
             *grads,
-            shape((2, 7, total, features), LOW),
             shape((2, 9, total, CHUNK), LOW),
             shape((2, 9, total, CHUNK), LOW),
         ]
-        out_specs = [vmem] * 5 + [anywhere] * 5
+        out_specs = [vmem] * 5 + [anywhere] * 4
     else:
         out_shape = [
             shape((2, 16, features), FULL),
@@ -1371,21 +1365,70 @@
             dma((4,)),
             dma((2, 9)),
             dma((2, 9)),
-            dma((2, 7)),
-            dma((2, 7)),
             dma((2, 2)),
             dma((9, 2)),
         ]
     return pl.pallas_call(
         functools.partial(backward_kernel, parts),
         out_shape=out_shape,
-        in_specs=[anywhere, anywhere, smem, smem, vmem, vmem] + [anywhere] * 15,
+        in_specs=[anywhere, anywhere, smem, smem, vmem, vmem] + [anywhere] * 16,
         out_specs=out_specs,
         scratch_shapes=scratch,
         compiler_params=pltpu.CompilerParams(
             collective_id=1, has_side_effects=True, vmem_limit_bytes=60 * 1024 * 1024
         ),
     )(cot_query, cot_passage, qlens, plens, gcls, par, *own, *land, *kept)
+
+
+def finish_kernel(parts, *refs):
+    big, vec, loss = refs[:8], refs[8], refs[9]
+    outs, small, total = refs[10:18], refs[18:26], refs[26]
+    held, come, go = refs[27:35], refs[35], refs[36]
+    copies = []
+    for src, mid, dst in zip(big, held, outs):
+        pieces = 2 if src.shape[0] % 32 == 0 or len(src.shape) == 3 else 1
+        size = src.shape[0] // pieces
+        for item in range(pieces):
+            rows, spot = pl.ds(item * size, size), len(copies)
+            copies.append(
+                (
+                    pltpu.make_async_copy(src.at[rows], mid.at[rows], come.at[spot]),
+                    pltpu.make_async_copy(mid.at[rows], dst.at[rows], go.at[spot]),
+                )
+            )
+            copies[-1][0].start()
+    me = lax.axis_index("batch")
+    features = vec.shape[1]
+    for at, count, out in zip((0, 2, 3, 4, 5, 9, 10, 11), (2, 1, 1, 1, 4, 1, 1, 1), small):
+        size = count * features // parts
+        every = parts // count
+        block = vec[pl.ds(at + me // every, 1)]
+        block = jnp.broadcast_to(block, (8, features))
+        turned = pltpu.roll(block, (features - size * (me % every)) % features, 1)
+        out[...] = turned[0:1, 0:size]
+    total[...] = loss[0:1, 0:1]
+    for came, left in copies:
+        came.wait()
+        left.start()
+    for came, left in copies:
+        left.wait()
+
+
+def finish(parts, big, vec, loss):
+    features = vec.shape[1]
+    anywhere = pl.BlockSpec(memory_space=pl.ANY)
+    vmem = pl.BlockSpec(memory_space=pltpu.VMEM)
+    shape = jax.ShapeDtypeStruct
+    return pl.pallas_call(
+        functools.partial(finish_kernel, parts),
+        out_shape=[shape(item.shape, item.dtype) for item in big]
+        + [shape((1, count * features // parts), FULL) for count in (2, 1, 1, 1, 4, 1, 1, 1)]
+        + [shape((1, 1), FULL)],
+        in_specs=[anywhere] * 8 + [vmem] * 2,
+        out_specs=[anywhere] * 8 + [vmem] * 9,
+        scratch_shapes=[pltpu.VMEM(item.shape, item.dtype) for item in big]
+        + [pltpu.SemaphoreType.DMA((16,)), pltpu.SemaphoreType.DMA((16,))],
+    )(*big, vec, loss)
 
 
 def per_device(
@@ -1406,7 +1449,7 @@
     vectors = [weights[item] for item in (1, 3, 4, 5, 7, 9, 10, 11)]
     features = x_query.shape[2]
     half_q, half_p = x_query.shape[0] // 2, x_passage.shape[0] // 2
-    *kept, par, l_qkv, l_o, l_in, l_out, hidden_q, hidden_p, grad_cls, loss = forward_both(
+    *kept, par, l_qkv, l_o, l_in, l_out, hidden_q, hidden_p, land_a, grad_cls, loss = forward_both(
         parts,
         x_query,
         x_passage.reshape(-1, QLEN, features),
@@ -1417,13 +1460,11 @@
         own,
     )
     other = (l_qkv, l_o, l_in, l_out)
-    hidden_q, hidden_p = hidden_q[None], hidden_p.reshape(x_passage.shape)[None]
-    if parts == 16:
-        loss_value = loss[0, 0]
-    else:
+    if parts != 16:
+        last = hidden_p.reshape(x_passage.shape)
         targets = lax.all_gather(positive, "batch", axis=0, tiled=True)
-        own_q = hidden_q[0, :, 0]
-        own_p = hidden_p[0, :, 0]
+        own_q = hidden_q[:, 0]
+        own_p = last[:, 0]
         last_q, last_p = (jnp.where(on_first, swap(item), item) for item in (own_q, own_p))
         cls_query = lax.all_gather(last_q, "batch", axis=0, tiled=True)
         cls_passage = lax.all_gather(last_p, "batch", axis=0, tiled=True)
@@ -1457,18 +1498,16 @@
         par,
         own,
         other,
-        kept,
+        kept + [land_a],
     )
     groups = ((0, 2), (2, 1), (3, 1), (4, 1), (5, 4), (9, 1), (10, 1), (11, 1))
     if parts == 16:
         d_qkv, d_o, d_in, d_out, d_vec, grad_q, grad_p = outs[:7]
-        d_out = d_out.reshape(-1, features)
-        batch = lax.axis_index("batch")
-        small = []
-        for at, count in groups:
-            flat = d_vec[at : at + count].reshape(-1)
-            size = flat.shape[0] // parts
-            small.append(lax.dynamic_slice_in_dim(flat, batch * size, size, 0))
+        big = (hidden_q, hidden_p, grad_q, grad_p, d_qkv, d_o, d_in, d_out.reshape(-1, features))
+        *final, loss = finish(parts, big, d_vec, loss)
+        hidden_q, hidden_p, grad_q, grad_p, d_qkv, d_o, d_in, d_out = final[:8]
+        small = [item[0] for item in final[8:]]
+        loss_value = loss.reshape(())
     else:
         sums, grad_q, grad_p, g_pro, g_att, g_up, g_flo = outs
         left = kept[0]
@@ -1495,6 +1534,7 @@
             total([sums[layer, at : at + count].reshape(-1) for layer in (0, 1)])
             for at, count in groups
         ]
+    hidden_q, hidden_p = hidden_q[None], hidden_p.reshape(x_passage.shape)[None]
     grad_q = grad_q[None]
     grad_p = grad_p.reshape(x_passage.shape)[None]
     d_b_qv, d_b_o, d_g_attn, d_c_attn, d_b_in, d_b_out, d_g_ffn, d_c_ffn = small

time: 232 us -> 224 us (0.966)
  local copies, waits for them, and re-layouts: 14.7 us -> 0 us
  Pallas kernels: 216 us -> 223 us
    unnamed x22 -> x0, local copies, waits for them, and re-layouts: 7.98 us -> none
    pallas_call x0 -> x1, Pallas kernels: none -> 6.48 us  [finish(): pl.pallas_call(functools.partial(finish_kernel, parts), out_shape=[shape(...]
    slice x4 -> x0, local copies, waits for them, and re-layouts: 3.72 us -> none  [the longest x3 2.53 us: per_device(): flat = d_vec[at:at + count].reshape(-1)]
    dynamic_slice x4 -> x0, local copies, waits for them, and re-layouts: 2.41 us -> none  [per_device(): small.append(lax.dynamic_slice_in_dim(flat, batch * size, size, 0))]
where the time goes in v1:
time: 224 us
  Pallas kernels  223 us (100%)
    pallas_call x1, Pallas kernels, backward_both(): pl.pallas_call(functools.partial(backward_kernel, parts), out_shape=out_s...  161 us
    pallas_call x1, Pallas kernels, forward_both(): pl.pallas_call(functools.partial(forward_kernel, parts), out_shape=[shape...  55.7 us
    pallas_call x1, Pallas kernels, finish(): pl.pallas_call(functools.partial(finish_kernel, parts), out_shape=[shape(...  6.48 us

profile of v1, /device:TPU:0, one launch (start us, length us, event | category | flops | bytes accessed | tf_op | source)
XLA Modules:
  0.0 224.0 jit_solution(14281279560237445439)
XLA Ops:
  0.7 55.7 %shard_map.314 = (bf16[2,7,384,768]{3,2,1,0:T(8,128)(2,1)}, bf16[2,384,2304]{2,1,0:T(8,128)(2,1)}, bf16[2,12,128,128]{3,2,1,0:T(8,128)(2,1)}, bf16[2,12,256,256]...) custom-call(bf16[8,32,768]{2,1,0:T(8,128)(2,1)} %x_query.1, ...), custom_call_target="tpu_custom_call" | custom-call | tf_op jit(solution)/shard_map/pallas_call | solution.py:557
  56.4 161.0 %shard_map.315 = (f32[48,2304]{1,0:T(8,128)}, f32[48,768]{1,0:T(8,128)}, f32[48,3072]{1,0:T(8,128)}, f32[4,48,768]{2,1,0:T(8,128)}, f32[16,768]{1,0:T(8,128)}, /...) custom-call(bf16[8,32,768]{2,1,0:T(8,128)(2,1)} %refs_0_.1, ...), custom_call_target="tpu_custom_call" | custom-call | tf_op jit(solution)/shard_map/pallas_call | solution.py:1371
  217.4 6.5 %shard_map.316 = (bf16[8,32,768]{2,1,0:T(8,128)(2,1)}, bf16[16,32,768]{2,1,0:T(8,128)(2,1)}, f32[8,32,768]{2,1,0:T(8,128)}, f32[16,32,768]{2,1,0:T(8,128)}, f32[...) custom-call(bf16[8,32,768]{2,1,0:T(8,128)(2,1)} %get-tuple-element.5, ...), custom_call_target="tpu_custom_call" | custom-call | tf_op jit(solution)/shard_map/pallas_call | solution.py:1422

commit v2 on v1

--- a/solution.py
+++ b/solution.py
@@ -603,6 +603,11 @@
     return [jnp.sum(item, 0, keepdims=True) for item in sums]
 
 
+LAGS = (2, 4, 6)
+RING = 12
+HELD = 8
+
+
 def left_index(ch):
     return (
         jnp.minimum(ch, 4) + (ch >= 8).astype(jnp.int32) + (ch >= 9).astype(jnp.int32)
@@ -632,7 +637,9 @@
     buffers = take(4)
     bqkv, bo, bin_, bout = buffers
     qkv, pq, pp, source, slope, gsrc = take(6)
-    attn_full, attn, steep, flow_full, flow, gmixed, grow = take(7)
+    attn_full, attn, steep, flow_full, flow = take(5)
+    gmixed = flow
+    grow = flow_full.reshape(flow.shape[0] // QLEN, QLEN, flow.shape[1])
     wload, fetch, cload, hsend, hrecv, hlocal, ksem = take(7)
     if small:
         vpar, a_buf, g_buf, stage, s1, r1, s2, r2, s3, r3 = take(10)
@@ -709,8 +716,29 @@
         target = (f_flo, f_up, f_att, f_pro)[slot]
         return pltpu.make_async_copy(ref, target.at[layer], ksem.at[slot])
 
+    def direct():
+        spot, ref, width, item = pieces_of(0)[0]
+        lanes = pl.ds(pl.multiple_of((1 - core) * width, 128), CHUNK)
+        return remote(
+            ref.at[:, lanes], g_buf.at[0, pl.ds(total, total)], gs.at[1, 0], gr.at[1, 0], peer
+        )
+
     def give(layer, slot):
-        if small:
+        if small and slot == 0:
+
+            @pl.when(layer == 1)
+            def _():
+                direct().start()
+                lanes = pl.ds(pl.multiple_of(core * CHUNK, 128), CHUNK)
+                g_buf[0, pl.ds(0, total)] = flow[:, lanes]
+
+            @pl.when(layer == 0)
+            def _():
+                piece = pieces_of(0)[0]
+                peer_piece(layer, piece).start()
+                own_piece(layer, piece).start()
+
+        elif small:
             for piece in pieces_of(slot):
                 peer_piece(layer, piece).start()
                 own_piece(layer, piece).start()
@@ -911,7 +939,7 @@
         sums[12:16] = jnp.zeros((4, features), FULL)
         weight_wait(0)
         rows_all = attn_full[...] + dot_last(qkv[...], bqkv[...])
-        grow[...] = rows_all.reshape(grow.shape)
+        flow_full[...] = rows_all
         gsrc[...] = rows_all.astype(LOW).reshape(gsrc.shape)
 
         @pl.when(core == layer)
@@ -980,7 +1008,6 @@
     for step in (1, 2, 3):
         other = ((z + step) % 4) * 4 + me % 4
         targets += [{"section": sec, "batch": other} for sec in (0, 1)]
-    greet(targets)
 
     def stage_copy(number, side):
         layer, spot = 1 - number // 7, number % 7
@@ -1009,9 +1036,19 @@
                     for item in range(4):
                         a_buf[item, spot, half, :, :, lanes] = shaped[:, item]
 
-        @pl.when(number + 2 < 14)
-        def _():
+        if isinstance(number, int):
             stage_start(number + 2)
+        else:
+
+            @pl.when(number + 2 < 14)
+            def _():
+                stage_start(number + 2)
+
+    stage_start(0)
+    stage_start(1)
+    for spot in range(4):
+        turn(spot, spot)
+    greet(targets)
 
     def right_copy(layer, spot, side):
         src = own_g if side == 0 else land_g
@@ -1023,7 +1060,7 @@
         ch = k % COUNT
         layer = 1 - k // COUNT
 
-        @pl.when((k < 2 * COUNT) & ((ch == 0) | (ch >= 4)))
+        @pl.when((k > 0) & (k < 2 * COUNT) & ((ch == 0) | (ch >= 4)))
         def _():
             spot = right_index(ch)
             right_copy(layer, spot, 0).start()
@@ -1033,17 +1070,15 @@
             ).wait_recv()
             right_copy(layer, spot, 1).start()
 
-    RING = 12
-
     def first(k, par_):
         return remote(
-            s1.at[k % 4], r1.at[k % RING], s1s.at[k], r1s.at[k],
+            s1.at[k % HELD], r1.at[k % RING], s1s.at[k], r1s.at[k],
             {"batch": px if par_ == 0 else py},
         )
 
     def second(k, par_):
         return remote(
-            s2.at[k % 4], r2.at[k % RING], s2s.at[k], r2s.at[k],
+            s2.at[k % 4], r2.at[k % HELD], s2s.at[k], r2s.at[k],
             {"batch": py if par_ == 0 else px},
         )
 
@@ -1071,7 +1106,7 @@
     def ready(k, par_):
         ch = k % COUNT
 
-        @pl.when((ch == 0) | (ch >= 4))
+        @pl.when((k > 0) & ((ch == 0) | (ch >= 4)))
         def _():
             for side in (0, 1):
                 right_copy(0, right_index(ch), side).wait()
@@ -1079,7 +1114,11 @@
         base = (k // COUNT) * 7
         if par_ == 0:
 
-            @pl.when(ch == 0)
+            @pl.when(k == 0)
+            def _():
+                direct().wait_recv()
+
+            @pl.when(k == COUNT)
             def _():
                 for spot in range(4):
                     turn(base + spot, spot)
@@ -1099,7 +1138,7 @@
         ready(k, par_)
         ref = left_of(k)
         block = ref[:, :, 1 - x] if par_ == 0 else ref[:, 1 - y]
-        s1[k % 4] = product(k, block, 8 * BLOCK).astype(LOW).reshape(4, 2, BLOCK, CHUNK)
+        s1[k % HELD] = product(k, block, 8 * BLOCK).astype(LOW).reshape(4, 2, BLOCK, CHUNK)
         first(k, par_).start()
 
     def part_two(k, par_):
@@ -1121,7 +1160,7 @@
         value = (
             product(k, ref[:, y, x], 4 * BLOCK).reshape(4, BLOCK, CHUNK)
             + came.astype(FULL)
-            + r2[k % RING].astype(FULL)
+            + r2[k % HELD].astype(FULL)
         )
         s3[k % 4] = value.astype(LOW)
         for step in (1, 2, 3):
@@ -1135,7 +1174,7 @@
         def _():
             r3[core, k % COUNT, z] = s3[k % 4, z]
 
-    def part_four(k):
+    def part_four(k, par_):
         layer = 1 - k // COUNT
         ch = k % COUNT
         for step in (1, 2, 3):
@@ -1182,17 +1221,19 @@
             {"batch": ((z + step) % 4) * 4 + me % 4},
         )
 
-    steps = 2 * COUNT + 6
+    steps = 2 * COUNT + LAGS[2]
+
+    starts = ((-1, 3), (0, 4), (1, 6), (2, 8))
 
     def pair(turn_index, carry):
         kk = turn_index - 1
         layer = (kk < 3).astype(jnp.int32)
 
-        for slot, (one, two) in enumerate(((0, 4), (1, 4), (2, 5), (3, 6))):
-
-            @pl.when((kk == one) | (kk == two))
+        for slot, (one, two) in enumerate(starts):
+
+            @pl.when((kk == one + 1) | (kk == two + 1))
             def _():
-                done = (kk == one).astype(jnp.int32)
+                done = (kk == one + 1).astype(jnp.int32)
                 given(done, slot)
                 reload(done, slot)
                 if slot == 3:
@@ -1200,73 +1241,66 @@
 
         @pl.when(kk == -1)
         def _():
-            stage_start(0)
-            stage_start(1)
             rest_of_loads()
             for copy in cots:
                 copy.wait()
 
         for par_ in (0, 1):
+            right_start(2 * kk + 2 + par_)
+
+        for par_ in (0, 1):
             k = 2 * kk + par_
-
-            @pl.when((k >= 0) & (k < 2 * COUNT))
+            for lag, part in zip(LAGS, (part_two, part_three, part_four)):
+
+                @pl.when((k >= lag) & (k < 2 * COUNT + lag))
+                def _():
+                    part(k - lag, par_)
+
+        for slot, (one, two) in enumerate(starts):
+            if slot == 0:
+
+                @pl.when((kk == one) | (kk == two))
+                def _():
+                    slots[slot](layer)
+
+        for par_ in (0, 1):
+            k = 2 * kk + 2 + par_
+
+            @pl.when(k < 2 * COUNT)
             def _():
                 part_one(k, par_)
 
-        for par_ in (0, 1):
-            k = 2 * kk + par_
-
-            @pl.when((k >= 2) & (k < 2 * COUNT + 2))
-            def _():
-                part_two(k - 2, par_)
-
-            @pl.when((k >= 4) & (k < 2 * COUNT + 4))
-            def _():
-                part_three(k - 4, par_)
-
-            @pl.when(k >= 6)
-            def _():
-                part_four(k - 6)
-
-        for slot, (one, two) in enumerate(((-1, 3), (0, 3), (1, 4), (2, 5))):
-
-            @pl.when((kk == one) | (kk == two))
-            def _():
-                slots[slot](layer)
-
-        @pl.when(kk == -1)
-        def _():
-            own_piece(1, pieces_of(0)[0]).wait()
-
-        @pl.when((kk >= -1) & (kk < COUNT - 1))
-        def _():
-            for par_ in (0, 1):
-                right_start(2 * kk + 2 + par_)
-
-        @pl.when(kk == 6)
+        for slot, (one, two) in enumerate(starts):
+            if slot > 0:
+
+                @pl.when((kk == one) | (kk == two))
+                def _():
+                    slots[slot](layer)
+
+        @pl.when(kk == 9)
         def _():
             vec_cross.start()
 
-        @pl.when(kk == 7)
+        @pl.when(kk == 10)
         def _():
             vec_cross.wait()
             va[...] = vpar[core] + ra[...]
             vec_x.start()
 
-        @pl.when(kk == 8)
+        @pl.when(kk == 11)
         def _():
             vec_x.wait()
             vb[...] = va[...] + rb[...]
             vec_y.start()
 
-        @pl.when(kk == 9)
+        @pl.when(kk == 12)
         def _():
             vec_y.wait()
             vc[...] = vb[...] + rc[...]
             for step in (1, 2, 3):
                 vec_z(step, z).start()
 
-        @pl.when(kk == 11)
+        @pl.when(kk == 14)
         def _():
             for step in (1, 2, 3):
                 vec_z(step, z).wait_send()
@@ -1327,8 +1361,6 @@
         pltpu.VMEM((2, total, 256), FULL),
         pltpu.VMEM((total, features), FULL),
         pltpu.VMEM((total, features), LOW),
-        pltpu.VMEM((total, features), LOW),
-        pltpu.VMEM((total // QLEN, QLEN, features), FULL),
         dma((4,)),
         dma((6,)),
         dma((2,)),
@@ -1345,10 +1377,10 @@
             pltpu.VMEM((7, 4, 2, 2, BLOCK, 2 * total), LOW),
             pltpu.VMEM((9, 2 * total, CHUNK), LOW),
             pltpu.VMEM((2, 2, total, features), LOW),
-            pltpu.VMEM((4, 4, 2, BLOCK, CHUNK), LOW),
-            pltpu.VMEM((12, 4, 2, BLOCK, CHUNK), LOW),
+            pltpu.VMEM((HELD, 4, 2, BLOCK, CHUNK), LOW),
+            pltpu.VMEM((RING, 4, 2, BLOCK, CHUNK), LOW),
             pltpu.VMEM((4, 4, BLOCK, CHUNK), LOW),
-            pltpu.VMEM((12, 4, BLOCK, CHUNK), LOW),
+            pltpu.VMEM((HELD, 4, BLOCK, CHUNK), LOW),
             pltpu.VMEM((4, 4, BLOCK, CHUNK), LOW),
             pltpu.VMEM((2, COUNT, 4, BLOCK, CHUNK), LOW),
             *[vector] * 6,

time: 224 us -> 214 us (0.955)
  Pallas kernels: 223 us -> 212 us
    pallas_call x1, Pallas kernels: 161 us -> 150 us  [backward_both(): pl.pallas_call(functools.partial(backward_kernel, parts), out_shape=out_s...]
where the time goes in v2:
time: 214 us; the launch traced here: 213 us
  Pallas kernels  212 us (99%)
    pallas_call x1, Pallas kernels, backward_both(): pl.pallas_call(functools.partial(backward_kernel, parts), out_shape=out_s...  150 us
    pallas_call x1, Pallas kernels, forward_both(): pl.pallas_call(functools.partial(forward_kernel, parts), out_shape=[shape...  55.9 us
    pallas_call x1, Pallas kernels, finish(): pl.pallas_call(functools.partial(finish_kernel, parts), out_shape=[shape(...  6.48 us

profile of v2, /device:TPU:0, one launch (start us, length us, event | category | flops | bytes accessed | tf_op | source)
XLA Modules:
  0.0 213.3 jit_solution(13714305167183120417)
XLA Ops:
  0.7 55.9 %shard_map.314 = (bf16[2,7,384,768]{3,2,1,0:T(8,128)(2,1)}, bf16[2,384,2304]{2,1,0:T(8,128)(2,1)}, bf16[2,12,128,128]{3,2,1,0:T(8,128)(2,1)}, bf16[2,12,256,256]...) custom-call(bf16[8,32,768]{2,1,0:T(8,128)(2,1)} %x_query.1, ...), custom_call_target="tpu_custom_call" | custom-call | tf_op jit(solution)/shard_map/pallas_call | solution.py:557
  56.5 150.1 %shard_map.315 = (f32[48,2304]{1,0:T(8,128)}, f32[48,768]{1,0:T(8,128)}, f32[48,3072]{1,0:T(8,128)}, f32[4,48,768]{2,1,0:T(8,128)}, f32[16,768]{1,0:T(8,128)}, /...) custom-call(bf16[8,32,768]{2,1,0:T(8,128)(2,1)} %refs_0_.1, ...), custom_call_target="tpu_custom_call" | custom-call | tf_op jit(solution)/shard_map/pallas_call | solution.py:1403
  206.7 6.5 %shard_map.316 = (bf16[8,32,768]{2,1,0:T(8,128)(2,1)}, bf16[16,32,768]{2,1,0:T(8,128)(2,1)}, f32[8,32,768]{2,1,0:T(8,128)}, f32[16,32,768]{2,1,0:T(8,128)}, f32[...) custom-call(bf16[8,32,768]{2,1,0:T(8,128)(2,1)} %get-tuple-element.5, ...), custom_call_target="tpu_custom_call" | custom-call | tf_op jit(solution)/shard_map/pallas_call | solution.py:1454

commit v3 on v2

--- a/solution.py
+++ b/solution.py
@@ -642,10 +642,10 @@
     grow = flow_full.reshape(flow.shape[0] // QLEN, QLEN, flow.shape[1])
     wload, fetch, cload, hsend, hrecv, hlocal, ksem = take(7)
     if small:
-        vpar, a_buf, g_buf, stage, s1, r1, s2, r2, s3, r3 = take(10)
+        vpar, a_buf, g_buf, stage, s1, r1, s2, r2, s3, r3, hold = take(11)
         va, ra, vb, rb, vc, rc, rz = take(7)
         s1s, r1s, s2s, r2s, s3s, r3s, vsend, vrecv, zsend, zrecv = take(10)
-        gs, gr, sl, gl = take(4)
+        gs, gr, sl, gl, el = take(5)
 
     core = lax.axis_index("section")
     me = lax.axis_index("batch")
@@ -686,6 +686,28 @@
             cot_passage.at[pl.ds(core * tall, tall)], gsrc.at[pl.ds(count_q, tall)], cload.at[1]
         ),
     ]
+    def early_copy(spot, side):
+        src = (left, land_a)[side]
+        if spot < 2:
+            dst, sem = stage.at[spot, side], sl.at[spot, side]
+        else:
+            lanes = pl.ds((spot - 2) * features, features)
+            dst, sem = bin_.at[pl.ds(side * total, total), lanes], el.at[spot - 2, side]
+        return pltpu.make_async_copy(src.at[1, spot], dst, sem)
+
+    if small:
+        x, y, z = me % 2, (me // 2) % 2, me // 4
+        px, py = me + 1 - 2 * x, me + 2 - 4 * y
+        targets = [{"batch": px}, {"batch": py}, peer]
+        for step in (1, 2, 3):
+            other = ((z + step) % 4) * 4 + me % 4
+            targets += [{"section": sec, "batch": other} for sec in (0, 1)]
+        barrier = pltpu.get_barrier_semaphore()
+        for where in targets:
+            pl.semaphore_signal(barrier, inc=1, device_id=where, device_id_type=MESH)
+        for spot in range(4):
+            for side in (0, 1):
+                early_copy(spot, side).start()
     saved_copy(1, 0).start()
     for copy in cots:
         copy.start()
@@ -1002,13 +1024,6 @@
         grads_came()
         return
 
-    x, y, z = me % 2, (me // 2) % 2, me // 4
-    px, py = me + 1 - 2 * x, me + 2 - 4 * y
-    targets = [{"batch": px}, {"batch": py}, peer]
-    for step in (1, 2, 3):
-        other = ((z + step) % 4) * 4 + me % 4
-        targets += [{"section": sec, "batch": other} for sec in (0, 1)]
-
     def stage_copy(number, side):
         layer, spot = 1 - number // 7, number % 7
         src = left if side == 0 else land_a
@@ -1020,13 +1035,11 @@
         stage_copy(number, 0).start()
         stage_copy(number, 1).start()
 
-    def turn(number, spot):
-        for side in (0, 1):
-            stage_copy(number, side).wait()
+    def rotate(spot, view):
         for side in (0, 1):
             lanes = pl.ds(side * total, total)
             for half in range(features // CHUNK):
-                block = stage[number % 2, side, :, pl.ds(half * CHUNK, CHUNK)].T
+                block = view(side, half * CHUNK).T
                 if spot > 3:
                     a_buf[spot, pl.ds(2 * half, 2), :, :, :, lanes] = block.reshape(
                         2, 2, 2, BLOCK, total
@@ -1036,19 +1049,29 @@
                     for item in range(4):
                         a_buf[item, spot, half, :, :, lanes] = shaped[:, item]
 
-        if isinstance(number, int):
+    def turn(number, spot):
+        for side in (0, 1):
+            stage_copy(number, side).wait()
+        rotate(spot, lambda side, at: stage[number % 2, side, :, pl.ds(at, CHUNK)])
+
+        @pl.when(number + 2 < 14)
+        def _():
             stage_start(number + 2)
+
+    for spot in range(4):
+        for side in (0, 1):
+            early_copy(spot, side).wait()
+        if spot < 2:
+            rotate(spot, lambda side, at: stage[spot, side, :, pl.ds(at, CHUNK)])
+            stage_start(spot + 4)
         else:
-
-            @pl.when(number + 2 < 14)
-            def _():
-                stage_start(number + 2)
-
-    stage_start(0)
-    stage_start(1)
-    for spot in range(4):
-        turn(spot, spot)
-    greet(targets)
+            rotate(
+                spot,
+                lambda side, at: bin_[
+                    pl.ds(side * total, total), pl.ds((spot - 2) * features + at, CHUNK)
+                ],
+            )
+    pl.semaphore_wait(barrier, len(targets))
 
     def right_copy(layer, spot, side):
         src = own_g if side == 0 else land_g
@@ -1142,26 +1165,23 @@
         first(k, par_).start()
 
     def part_two(k, par_):
+        ref = left_of(k)
+        block = ref[:, 1 - y, x] if par_ == 0 else ref[:, y, 1 - x]
+        hold[...] = product(k, block, 4 * BLOCK).reshape(4, BLOCK, CHUNK)
         first(k, par_).wait()
-        ref = left_of(k)
-        if par_ == 0:
-            block, came = ref[:, 1 - y, x], r1[k % RING, :, 1 - y]
-        else:
-            block, came = ref[:, y, 1 - x], r1[k % RING, :, 1 - x]
-        value = product(k, block, 4 * BLOCK).reshape(4, BLOCK, CHUNK) + came.astype(FULL)
-        s2[k % 4] = value.astype(LOW)
+        came = r1[k % RING, :, 1 - y] if par_ == 0 else r1[k % RING, :, 1 - x]
+        s2[k % 4] = (hold[...] + came.astype(FULL)).astype(LOW)
         second(k, par_).start()
 
     def part_three(k, par_):
-        second(k, par_).wait()
         layer = 1 - k // COUNT
         ref = left_of(k)
         came = r1[k % RING, :, y] if par_ == 0 else r1[k % RING, :, x]
-        value = (
-            product(k, ref[:, y, x], 4 * BLOCK).reshape(4, BLOCK, CHUNK)
-            + came.astype(FULL)
-            + r2[k % HELD].astype(FULL)
-        )
+        hold[...] = product(k, ref[:, y, x], 4 * BLOCK).reshape(
+            4, BLOCK, CHUNK
+        ) + came.astype(FULL)
+        second(k, par_).wait()
+        value = hold[...] + r2[k % HELD].astype(FULL)
         s3[k % 4] = value.astype(LOW)
         for step in (1, 2, 3):
             third(k, step).start()
@@ -1248,20 +1268,23 @@
         for par_ in (0, 1):
             right_start(2 * kk + 2 + par_)
 
-        for par_ in (0, 1):
-            k = 2 * kk + par_
-            for lag, part in zip(LAGS, (part_two, part_three, part_four)):
+        stages = (part_two, part_three, part_four)
+
+        def advance(item):
+            lag, part = LAGS[item], stages[item]
+            for par_ in (0, 1):
+                k = 2 * kk + par_
 
                 @pl.when((k >= lag) & (k < 2 * COUNT + lag))
                 def _():
                     part(k - lag, par_)
 
-        for slot, (one, two) in enumerate(starts):
-            if slot == 0:
-
-                @pl.when((kk == one) | (kk == two))
-                def _():
-                    slots[slot](layer)
+        advance(0)
+        advance(1)
+
+        @pl.when((kk == starts[0][0]) | (kk == starts[0][1]))
+        def _():
+            slots[0](layer)
 
         for par_ in (0, 1):
             k = 2 * kk + 2 + par_
@@ -1269,6 +1292,8 @@
             @pl.when(k < 2 * COUNT)
             def _():
                 part_one(k, par_)
+
+        advance(2)
 
         for slot, (one, two) in enumerate(starts):
             if slot > 0:
@@ -1383,6 +1408,7 @@
             pltpu.VMEM((HELD, 4, BLOCK, CHUNK), LOW),
             pltpu.VMEM((4, 4, BLOCK, CHUNK), LOW),
             pltpu.VMEM((2, COUNT, 4, BLOCK, CHUNK), LOW),
+            pltpu.VMEM((4, BLOCK, CHUNK), FULL),
             *[vector] * 6,
             pltpu.VMEM((4, 16, features), FULL),
             dma((steps,)),
@@ -1399,6 +1425,7 @@
             dma((2, 9)),
             dma((2, 2)),
             dma((9, 2)),
+            dma((2, 2)),
         ]
     return pl.pallas_call(
         functools.partial(backward_kernel, parts),

time: 214 us -> 208 us (0.972)
  Pallas kernels: 212 us -> 207 us
    pallas_call x1, Pallas kernels: 150 us -> 144 us  [backward_both(): pl.pallas_call(functools.partial(backward_kernel, parts), out_shape=out_s...]
where the time goes in v3:
time: 208 us; the launch traced here: 207 us
  Pallas kernels  207 us (100%)
    pallas_call x1, Pallas kernels, backward_both(): pl.pallas_call(functools.partial(backward_kernel, parts), out_shape=out_s...  144 us
    pallas_call x1, Pallas kernels, forward_both(): pl.pallas_call(functools.partial(forward_kernel, parts), out_shape=[shape...  55.9 us
    pallas_call x1, Pallas kernels, finish(): pl.pallas_call(functools.partial(finish_kernel, parts), out_shape=[shape(...  6.48 us

profile of v3, /device:TPU:0, one launch (start us, length us, event | category | flops | bytes accessed | tf_op | source)
XLA Modules:
  0.0 207.4 jit_solution(16338454396220950940)
XLA Ops:
  0.7 55.9 %shard_map.314 = (bf16[2,7,384,768]{3,2,1,0:T(8,128)(2,1)}, bf16[2,384,2304]{2,1,0:T(8,128)(2,1)}, bf16[2,12,128,128]{3,2,1,0:T(8,128)(2,1)}, bf16[2,12,256,256]...) custom-call(bf16[8,32,768]{2,1,0:T(8,128)(2,1)} %x_query.1, ...), custom_call_target="tpu_custom_call" | custom-call | tf_op jit(solution)/shard_map/pallas_call | solution.py:557
  56.5 144.2 %shard_map.315 = (f32[48,2304]{1,0:T(8,128)}, f32[48,768]{1,0:T(8,128)}, f32[48,3072]{1,0:T(8,128)}, f32[4,48,768]{2,1,0:T(8,128)}, f32[16,768]{1,0:T(8,128)}, /...) custom-call(bf16[8,32,768]{2,1,0:T(8,128)(2,1)} %refs_0_.1, ...), custom_call_target="tpu_custom_call" | custom-call | tf_op jit(solution)/shard_map/pallas_call | solution.py:1430
  200.7 6.5 %shard_map.316 = (bf16[8,32,768]{2,1,0:T(8,128)(2,1)}, bf16[16,32,768]{2,1,0:T(8,128)(2,1)}, f32[8,32,768]{2,1,0:T(8,128)}, f32[16,32,768]{2,1,0:T(8,128)}, f32[...) custom-call(bf16[8,32,768]{2,1,0:T(8,128)(2,1)} %get-tuple-element.5, ...), custom_call_target="tpu_custom_call" | custom-call | tf_op jit(solution)/shard_map/pallas_call | solution.py:1481

commit v4 on v3

--- a/solution.py
+++ b/solution.py
@@ -135,7 +135,7 @@
     l_qkv, l_o, l_in, l_out, hid_q, hid_p, land_a, gcls, loss,
     tok, out, bqkv, bo, bin_, bout, qkv, pq, pp, mixed, pre, normed_full, normed, up, act,
     slope, ffn, rows8, rows48, packed, every, stack,
-    load, save, xload, parsend, parrecv, wsend, wrecv, hsend, hrecv, hlocal, gsend, grecv, psend, precv, asend, arecv,
+    load, save, xload, parsend, parrecv, wsend, wrecv, hsend, hrecv, hlocal, gsend, grecv, psend, precv, asend, arecv, bsend, brecv,
 ):
     core = lax.axis_index("section")
     me = lax.axis_index("batch")
@@ -169,6 +169,21 @@
     def give_first(spot):
         return remote(own[spot], buffers[spot], wsend.at[spot], wrecv.at[spot], peer)
 
+    def give_block(spot, block):
+        part = pl.ds(block * features, features)
+        cut = (slice(None), part) if spot == 2 else (part,)
+        return remote(
+            own[spot].at[cut], buffers[spot].at[cut],
+            bsend.at[spot - 2, block], brecv.at[spot - 2, block], peer,
+        )
+
+    def weight_block(spot, block):
+        @pl.when(core == 1)
+        def _():
+            give_block(spot, block).wait_recv()
+            if block == 3:
+                stash(spot).start()
+
     def give_second(spot):
         return remote(own[spot], land[spot], wsend.at[spot], wrecv.at[spot], peer)
 
@@ -195,8 +210,11 @@
 
     @pl.when(core == 0)
     def _():
-        for spot in range(4):
+        for spot in range(2):
             give_first(spot).start()
+        for spot in (2, 3):
+            for block in range(4):
+                give_block(spot, block).start()
 
     @pl.when(core == 1)
     def _():
@@ -210,8 +228,12 @@
 
         @pl.when(core == 1)
         def _():
-            give_first(spot).wait_recv()
-            stash(spot).start()
+            if spot < 2:
+                give_first(spot).wait_recv()
+                stash(spot).start()
+
+        if spot >= 2:
+            weight_block(spot, 0)
 
     def fetch_second(spot):
         @pl.when(core == 0)
@@ -344,7 +366,7 @@
             normed_full[rows] = block
             normed[rows] = block.astype(LOW)
 
-        over(total // ROWS, norm_one, UNROLL)
+        over(total // ROWS, norm_one, 12)
         keep_left("normed", layer, normed)
         weight(layer, 2)
         free("slope", layer)
@@ -370,10 +392,13 @@
         expand(0)
 
         def grow(index):
+            if layer == 0 and (index + 1) % 3 == 0:
+                weight_block(2, (index + 1) // 3)
             expand(index + 1)
             bend(index)
 
-        over(tiles - 1, grow)
+        for index in range(tiles - 1):
+            grow(index)
         bend(tiles - 1)
         for item in range(4):
             lanes = pl.ds(item * features, features)
@@ -381,9 +406,16 @@
         keep("slope", layer, slope, o_slope.at[layer])
         weight(layer, 3)
         free("ffn", layer)
-        ffn[...] = (
-            dot(act[...], bout[...]) + normed_full[...] + par[base_row + 9 : base_row + 10]
-        )
+        ends = normed_full[...] + par[base_row + 9 : base_row + 10]
+        if layer == 0:
+            most = 3 * features
+            for block in (1, 2):
+                weight_block(3, block)
+            ffn[...] = dot(act[:, :most], bout[:most]) + ends
+            weight_block(3, 3)
+            ffn[...] += dot(act[:, most:], bout[most:])
+        else:
+            ffn[...] = dot(act[...], bout[...]) + ends
         keep("ffn", layer, ffn, o_ffn.at[layer])
         if layer == 0:
             fetch_second(2)
@@ -395,7 +427,7 @@
             block = moments(ffn[rows])[0] * par[base_row + 10 : base_row + 11]
             flat[rows] = (block + par[base_row + 11 : base_row + 12]).astype(LOW)
 
-        over(total // ROWS, norm_two, UNROLL)
+        over(total // ROWS, norm_two, 12)
         sides = (
             (target.at[pl.ds(0, count_q)], hid_q.at[pl.ds(core * count_q, count_q)]),
             (target.at[pl.ds(count_q, tall)], hid_p.at[pl.ds(core * tall, tall)]),
@@ -482,8 +514,19 @@
     )
     for spot, (src, dst) in enumerate(zip((item[0] for item in sides), theirs)):
         remote(src, dst, hsend.at[spot], hrecv.at[spot], peer).wait()
-    for spot in range(4):
-        give_second(spot).wait_send()
+    @pl.when(core == 0)
+    def _():
+        for spot in range(2):
+            give_first(spot).wait_send()
+        for spot in (2, 3):
+            for block in range(4):
+                give_block(spot, block).wait_send()
+
+    @pl.when(core == 1)
+    def _():
+        for spot in range(4):
+            give_second(spot).wait_send()
+
     give_par.wait_send()
     for (name, layer), copy in saves.items():
         if layer == 1:
@@ -553,6 +596,8 @@
         dma,
         dma((2, 7)),
         dma((2, 7)),
+        dma((2, 4)),
+        dma((2, 4)),
     ]
     return pl.pallas_call(
         functools.partial(forward_kernel, parts),
@@ -1445,17 +1490,14 @@
     held, come, go = refs[27:35], refs[35], refs[36]
     copies = []
     for src, mid, dst in zip(big, held, outs):
-        pieces = 2 if src.shape[0] % 32 == 0 or len(src.shape) == 3 else 1
-        size = src.shape[0] // pieces
-        for item in range(pieces):
-            rows, spot = pl.ds(item * size, size), len(copies)
-            copies.append(
-                (
-                    pltpu.make_async_copy(src.at[rows], mid.at[rows], come.at[spot]),
-                    pltpu.make_async_copy(mid.at[rows], dst.at[rows], go.at[spot]),
-                )
+        spot = len(copies)
+        copies.append(
+            (
+                pltpu.make_async_copy(src, mid, come.at[spot]),
+                pltpu.make_async_copy(mid, dst, go.at[spot]),
             )
-            copies[-1][0].start()
+        )
+        copies[-1][0].start()
     me = lax.axis_index("batch")
     features = vec.shape[1]
     for at, count, out in zip((0, 2, 3, 4, 5, 9, 10, 11), (2, 1, 1, 1, 4, 1, 1, 1), small):
@@ -1486,7 +1528,7 @@
         in_specs=[anywhere] * 8 + [vmem] * 2,
         out_specs=[anywhere] * 8 + [vmem] * 9,
         scratch_shapes=[pltpu.VMEM(item.shape, item.dtype) for item in big]
-        + [pltpu.SemaphoreType.DMA((16,)), pltpu.SemaphoreType.DMA((16,))],
+        + [pltpu.SemaphoreType.DMA((8,)), pltpu.SemaphoreType.DMA((8,))],
     )(*big, vec, loss)
 
 

time: 208 us -> 203 us (0.976)
  Pallas kernels: 207 us -> 202 us
    pallas_call x1, Pallas kernels: 55.9 us -> 51.8 us  [forward_both(): pl.pallas_call(functools.partial(forward_kernel, parts), out_shape=[shape...]
where the time goes in v4:
time: 203 us
  Pallas kernels  202 us (100%)
    pallas_call x1, Pallas kernels, backward_both(): pl.pallas_call(functools.partial(backward_kernel, parts), out_shape=out_s...  144 us
    pallas_call x1, Pallas kernels, forward_both(): pl.pallas_call(functools.partial(forward_kernel, parts), out_shape=[shape...  51.8 us
    pallas_call x1, Pallas kernels, finish(): pl.pallas_call(functools.partial(finish_kernel, parts), out_shape=[shape(...  5.97 us

profile of v4, /device:TPU:0, one launch (start us, length us, event | category | flops | bytes accessed | tf_op | source)
XLA Modules:
  0.0 203.1 jit_solution(11627382179036682928)
XLA Ops:
  0.7 51.8 %shard_map.314 = (bf16[2,7,384,768]{3,2,1,0:T(8,128)(2,1)}, bf16[2,384,2304]{2,1,0:T(8,128)(2,1)}, bf16[2,12,128,128]{3,2,1,0:T(8,128)(2,1)}, bf16[2,12,256,256]...) custom-call(bf16[8,32,768]{2,1,0:T(8,128)(2,1)} %x_query.1, ...), custom_call_target="tpu_custom_call" | custom-call | tf_op jit(solution)/shard_map/pallas_call | solution.py:602
  52.5 144.4 %shard_map.315 = (f32[48,2304]{1,0:T(8,128)}, f32[48,768]{1,0:T(8,128)}, f32[48,3072]{1,0:T(8,128)}, f32[4,48,768]{2,1,0:T(8,128)}, f32[16,768]{1,0:T(8,128)}, /...) custom-call(bf16[8,32,768]{2,1,0:T(8,128)(2,1)} %refs_0_.1, ...), custom_call_target="tpu_custom_call" | custom-call | tf_op jit(solution)/shard_map/pallas_call | solution.py:1475
  196.9 6.0 %shard_map.316 = (bf16[8,32,768]{2,1,0:T(8,128)(2,1)}, bf16[16,32,768]{2,1,0:T(8,128)(2,1)}, f32[8,32,768]{2,1,0:T(8,128)}, f32[16,32,768]{2,1,0:T(8,128)}, f32[...) custom-call(bf16[8,32,768]{2,1,0:T(8,128)(2,1)} %get-tuple-element.5, ...), custom_call_target="tpu_custom_call" | custom-call | tf_op jit(solution)/shard_map/pallas_call | solution.py:1523

commit v5 on v4

--- a/solution.py
+++ b/solution.py
@@ -1288,7 +1288,7 @@
 
     steps = 2 * COUNT + LAGS[2]
 
-    starts = ((-1, 3), (0, 4), (1, 6), (2, 8))
+    starts = ((-1, 3), (0, 4), (1, 5), (2, 6))
 
     def pair(turn_index, carry):
         kk = turn_index - 1
@@ -1347,30 +1347,30 @@
                 def _():
                     slots[slot](layer)
 
-        @pl.when(kk == 9)
+        @pl.when(kk == 7)
         def _():
             vec_cross.start()
 
-        @pl.when(kk == 10)
+        @pl.when(kk == 8)
         def _():
             vec_cross.wait()
             va[...] = vpar[core] + ra[...]
             vec_x.start()
 
-        @pl.when(kk == 11)
+        @pl.when(kk == 9)
         def _():
             vec_x.wait()
             vb[...] = va[...] + rb[...]
             vec_y.start()
 
-        @pl.when(kk == 12)
+        @pl.when(kk == 10)
         def _():
             vec_y.wait()
             vc[...] = vb[...] + rc[...]
             for step in (1, 2, 3):
                 vec_z(step, z).start()
 
-        @pl.when(kk == 14)
+        @pl.when(kk == 12)
         def _():
             for step in (1, 2, 3):
                 vec_z(step, z).wait_send()

time: 203 us -> 201 us (level)
  Pallas kernels: 202 us -> 199 us
    pallas_call x1, Pallas kernels: 144 us -> 142 us  [backward_both(): pl.pallas_call(functools.partial(backward_kernel, parts), out_shape=out_s...]
where the time goes in v5:
time: 201 us; the launch traced here: 200 us
  Pallas kernels  199 us (99%)
    pallas_call x1, Pallas kernels, backward_both(): pl.pallas_call(functools.partial(backward_kernel, parts), out_shape=out_s...  142 us
    pallas_call x1, Pallas kernels, forward_both(): pl.pallas_call(functools.partial(forward_kernel, parts), out_shape=[shape...  51.8 us
    pallas_call x1, Pallas kernels, finish(): pl.pallas_call(functools.partial(finish_kernel, parts), out_shape=[shape(...  5.97 us

profile of v5, /device:TPU:0, one launch (start us, length us, event | category | flops | bytes accessed | tf_op | source)
XLA Modules:
  0.0 200.2 jit_solution(4068544163805141085)
XLA Ops:
  0.7 51.8 %shard_map.314 = (bf16[2,7,384,768]{3,2,1,0:T(8,128)(2,1)}, bf16[2,384,2304]{2,1,0:T(8,128)(2,1)}, bf16[2,12,128,128]{3,2,1,0:T(8,128)(2,1)}, bf16[2,12,256,256]...) custom-call(bf16[8,32,768]{2,1,0:T(8,128)(2,1)} %x_query.1, ...), custom_call_target="tpu_custom_call" | custom-call | tf_op jit(solution)/shard_map/pallas_call | solution.py:602
  52.5 141.5 %shard_map.315 = (f32[48,2304]{1,0:T(8,128)}, f32[48,768]{1,0:T(8,128)}, f32[48,3072]{1,0:T(8,128)}, f32[4,48,768]{2,1,0:T(8,128)}, f32[16,768]{1,0:T(8,128)}, /...) custom-call(bf16[8,32,768]{2,1,0:T(8,128)(2,1)} %refs_0_.1, ...), custom_call_target="tpu_custom_call" | custom-call | tf_op jit(solution)/shard_map/pallas_call | solution.py:1475
  194.0 6.0 %shard_map.316 = (bf16[8,32,768]{2,1,0:T(8,128)(2,1)}, bf16[16,32,768]{2,1,0:T(8,128)(2,1)}, f32[8,32,768]{2,1,0:T(8,128)}, f32[16,32,768]{2,1,0:T(8,128)}, f32[...) custom-call(bf16[8,32,768]{2,1,0:T(8,128)(2,1)} %get-tuple-element.5, ...), custom_call_target="tpu_custom_call" | custom-call | tf_op jit(solution)/shard_map/pallas_call | solution.py:1523
